TPU v7x, 128 devices: a whole 4x4x4 slice. The times are simulated.
128 devices in a mesh: rep: 32 (over z, y, x_lo), shard: 4 (over x_hi, core).
Axes of the slice: x: 4 (x_hi: 2, x_lo: 2; x = x_hi * 2 + x_lo), y: 4, z: 4, core: 2. Of those that a mesh axis runs over, the one named last changes fastest.
Arguments:
- inputs: bfloat16 [1536, 197, 384], P(('rep', 'shard')), may hold values from -6 to 6
- out_grad: bfloat16 [1536, 197, 384], P(('rep', 'shard')), may hold values from -6 to 6
- ln1_gain: bfloat16 [384], P('shard'), may hold values from 0.099609375 to 1.8984375
- ln1_shift: bfloat16 [384], P('shard'), may hold values from -3 to 3
- qkv_weight: bfloat16 [384, 1152], P('shard'), may hold values from -0.3125 to 0.3125
- qv_bias: bfloat16 [768], P('shard'), may hold values from -3 to 3
- out_weight: bfloat16 [384, 384], P('shard'), may hold values from -1.25 to 1.25
- out_bias: bfloat16 [384], P('shard'), may hold values from -3 to 3
- ln2_gain: bfloat16 [384], P('shard'), may hold values from 0.099609375 to 1.8984375
- ln2_shift: bfloat16 [384], P('shard'), may hold values from -3 to 3
- up_weight: bfloat16 [384, 1536], P('shard'), may hold values from -0.3125 to 0.3125
- up_bias: bfloat16 [1536], P('shard'), may hold values from -3 to 3
- down_weight: bfloat16 [1536, 384], P('shard'), may hold values from -0.15625 to 0.15625
- down_bias: bfloat16 [384], P('shard'), may hold values from -3 to 3
Outputs:
- outputs: bfloat16 [1536, 197, 384], P(('rep', 'shard'))
- input_grad: bfloat16 [1536, 197, 384], P(('rep', 'shard'))
- ln1_gain_grad: float32 [384], P('shard')
- ln1_shift_grad: float32 [384], P('shard')
- qkv_weight_grad: float32 [384, 1152], P('shard')
- qv_bias_grad: float32 [768], P('shard')
- out_weight_grad: float32 [384, 384], P('shard')
- out_bias_grad: float32 [384], P('shard')
- ln2_gain_grad: float32 [384], P('shard')
- ln2_shift_grad: float32 [384], P('shard')
- up_weight_grad: float32 [384, 1536], P('shard')
- up_bias_grad: float32 [1536], P('shard')
- down_weight_grad: float32 [1536, 384], P('shard')
- down_bias_grad: float32 [384], P('shard')
All inputs are finite; a program needn't handle non-finite values.
Results may differ from a plain program's by a relative error of at most 0.029.
Values may be sent and summed in bfloat16 or wider, within the bound.
A program may use at most 256 MiB of HBM per device.

v0:
```python
from functools import partial

import jax
import jax.numpy as jnp
from jax import lax
from jax.sharding import PartitionSpec as P

HEADS = 6
HEAD_DIM = 64


def in_one_piece(arrays, axis, dim, along):
    columns = [a.reshape(*a.shape[:along], -1) for a in arrays]
    both = jnp.concatenate(columns, axis=along)
    result, at, done = (lax.all_gather(both, axis, axis=dim, tiled=True), 0, [])
    for a, column in zip(arrays, columns):
        section = result[..., at : at + column.shape[along]]
        done.append(section.reshape(*section.shape[:along], *a.shape[along:]))
        at += column.shape[along]
    return tuple(done)


def sent_together(arrays, axis, dim, along):
    columns = [a.reshape(*a.shape[:along], -1) for a in arrays]
    both = jnp.concatenate(columns, axis=along)
    result, at, done = (lax.psum_scatter(both, axis, scatter_dimension=dim, tiled=True), 0, [])
    for a, column in zip(arrays, columns):
        section = result[..., at : at + column.shape[along]]
        done.append(section.reshape(*section.shape[:along], *a.shape[along:]))
        at += column.shape[along]
    return tuple(done)


def layer_norm(values, gain_vec, shift_vec):
    average = jnp.mean(values, axis=-1, keepdims=True)
    centred = values - average
    variance = jnp.mean(centred * centred, axis=-1, keepdims=True)
    return centred * lax.rsqrt(variance + 1e-06) * gain_vec.astype(jnp.float32) + shift_vec.astype(
        jnp.float32
    )


def local(
    inputs,
    out_grad,
    ln1_gain,
    ln1_shift,
    qkv_weight,
    qv_bias,
    out_weight,
    out_bias,
    ln2_gain,
    ln2_shift,
    up_weight,
    up_bias,
    down_weight,
    down_bias,
):
    fwd_params = (
        lax.all_gather(ln1_gain, "shard", axis=0, tiled=True),
        *in_one_piece((ln1_shift, qkv_weight), "shard", 0, 1),
        lax.all_gather(qv_bias, "shard", axis=0, tiled=True),
        *in_one_piece((out_weight, out_bias, ln2_gain, ln2_shift, up_weight), "shard", 0, 1),
        *in_one_piece((up_bias, down_weight), "shard", 0, 1),
        lax.all_gather(down_bias, "shard", axis=0, tiled=True),
    )
    (
        gain_one,
        shift_one,
        qkv_full,
        qv_full,
        outw_full,
        outb_full,
        gain_two,
        shift_two,
        upw_full,
        upb_full,
        downw_full,
        downb_full,
    ) = fwd_params
    images, length, width = inputs.shape
    tokens = images * length
    score_scale = HEAD_DIM ** (-0.5)

    def heads_view(tensor):
        return tensor.reshape(images, length, HEADS, HEAD_DIM)

    flat_in = inputs.reshape(tokens, width).astype(jnp.float32)
    normed_one = layer_norm(flat_in, gain_one, shift_one).astype(jnp.bfloat16)
    packed = jnp.dot(normed_one, qkv_full, preferred_element_type=jnp.float32)
    qv_float = qv_full.astype(jnp.float32)
    query = heads_view((packed[:, :width] + qv_float[:width]).astype(jnp.bfloat16))
    key_rows = heads_view(packed[:, width : 2 * width].astype(jnp.bfloat16))
    value_rows = heads_view((packed[:, 2 * width :] + qv_float[width:]).astype(jnp.bfloat16))
    scores = (
        jnp.einsum("bqhe,bkhe->bhqk", query, key_rows, preferred_element_type=jnp.float32)
        * score_scale
    )
    peak = jnp.max(scores, axis=-1, keepdims=True)
    expo = jnp.exp(scores - peak)
    totals = jnp.sum(expo, axis=-1, keepdims=True)
    log_total = peak + jnp.log(totals)
    probs = (expo / totals).astype(jnp.bfloat16)
    mixed = jnp.einsum("bhqk,bkhe->bqhe", probs, value_rows, preferred_element_type=jnp.float32)
    mixed = mixed.reshape(tokens, width).astype(jnp.bfloat16)
    middle = (
        flat_in
        + jnp.dot(mixed, outw_full, preferred_element_type=jnp.float32)
        + outb_full.astype(jnp.float32)
    )
    normed_two = layer_norm(middle, gain_two, shift_two).astype(jnp.bfloat16)
    hidden_pre = jnp.dot(
        normed_two, upw_full, preferred_element_type=jnp.float32
    ) + upb_full.astype(jnp.float32)
    activated = jax.nn.gelu(hidden_pre, approximate=False).astype(jnp.bfloat16)
    result = (
        middle
        + jnp.dot(activated, downw_full, preferred_element_type=jnp.float32)
        + downb_full.astype(jnp.float32)
    )
    outputs = result.astype(jnp.bfloat16).reshape(images, length, width)
    back_params = (
        lax.all_gather(ln1_gain, "shard", axis=0, tiled=True),
        *in_one_piece((ln1_shift, qkv_weight), "shard", 0, 1),
        lax.all_gather(qv_bias, "shard", axis=0, tiled=True),
        *in_one_piece((out_weight, out_bias, ln2_gain, ln2_shift, up_weight), "shard", 0, 1),
        *in_one_piece((up_bias, down_weight), "shard", 0, 1),
        lax.all_gather(down_bias, "shard", axis=0, tiled=True),
    )
    (
        gain_one_b,
        shift_one_b,
        qkv_back,
        qv_back,
        outw_back,
        outb_back,
        gain_two_b,
        shift_two_b,
        upw_back,
        upb_back,
        downw_back,
        downb_back,
    ) = back_params
    cotangent = out_grad.reshape(tokens, width)
    cot_float = cotangent.astype(jnp.float32)
    down_w_grad = jnp.einsum("tf,td->fd", activated, cotangent, preferred_element_type=jnp.float32)
    down_b_grad = jnp.sum(cot_float, axis=0)
    act_grad = jnp.einsum("td,fd->tf", cotangent, downw_back, preferred_element_type=jnp.float32)
    _, gelu_back = jax.vjp(partial(jax.nn.gelu, approximate=False), hidden_pre)
    pre_grad = gelu_back(act_grad)[0].astype(jnp.bfloat16)
    up_w_grad = jnp.einsum("td,tf->df", normed_two, pre_grad, preferred_element_type=jnp.float32)
    up_b_grad = jnp.sum(pre_grad, axis=0, dtype=jnp.float32)
    norm_two_grad = jnp.einsum("tf,df->td", pre_grad, upw_back, preferred_element_type=jnp.float32)
    _, second_back = jax.vjp(
        layer_norm, middle, gain_two_b.astype(jnp.float32), shift_two_b.astype(jnp.float32)
    )
    mid_norm_grad, gain_two_grad, shift_two_grad = second_back(norm_two_grad)
    middle_grad = cot_float + mid_norm_grad
    branch_grad = middle_grad.astype(jnp.bfloat16)
    out_w_grad = jnp.einsum("td,te->de", mixed, branch_grad, preferred_element_type=jnp.float32)
    out_b_grad = jnp.sum(branch_grad, axis=0, dtype=jnp.float32)
    mixed_grad = jnp.einsum("te,de->td", branch_grad, outw_back, preferred_element_type=jnp.float32)
    mixed_grad = heads_view(mixed_grad.astype(jnp.bfloat16))
    again = (
        jnp.einsum("bqhe,bkhe->bhqk", query, key_rows, preferred_element_type=jnp.float32)
        * score_scale
    )
    probs_float = jnp.exp(again - log_total)
    probs_low = probs_float.astype(jnp.bfloat16)
    value_grad = jnp.einsum(
        "bhqk,bqhe->bkhe", probs_low, mixed_grad, preferred_element_type=jnp.float32
    )
    prob_grad = jnp.einsum(
        "bqhe,bkhe->bhqk", mixed_grad, value_rows, preferred_element_type=jnp.float32
    )
    inner = jnp.sum(probs_float * prob_grad, axis=-1, keepdims=True)
    score_grad = (probs_float * (prob_grad - inner)).astype(jnp.bfloat16)
    query_grad = (
        jnp.einsum("bhqk,bkhe->bqhe", score_grad, key_rows, preferred_element_type=jnp.float32)
        * score_scale
    )
    key_grad = (
        jnp.einsum("bhqk,bqhe->bkhe", score_grad, query, preferred_element_type=jnp.float32)
        * score_scale
    )
    packed_grad = jnp.concatenate(
        (
            query_grad.reshape(tokens, width),
            key_grad.reshape(tokens, width),
            value_grad.reshape(tokens, width),
        ),
        axis=1,
    ).astype(jnp.bfloat16)
    qkv_w_grad = jnp.einsum(
        "td,te->de", normed_one, packed_grad, preferred_element_type=jnp.float32
    )
    qv_b_grad = jnp.concatenate(
        (
            jnp.sum(packed_grad[:, :width], axis=0, dtype=jnp.float32),
            jnp.sum(packed_grad[:, 2 * width :], axis=0, dtype=jnp.float32),
        )
    )
    norm_one_grad = jnp.einsum(
        "te,de->td", packed_grad, qkv_back, preferred_element_type=jnp.float32
    )
    _, first_back = jax.vjp(
        layer_norm, flat_in, gain_one_b.astype(jnp.float32), shift_one_b.astype(jnp.float32)
    )
    in_norm_grad, gain_one_grad, shift_one_grad = first_back(norm_one_grad)
    input_grad = (middle_grad + in_norm_grad).astype(jnp.bfloat16).reshape(images, length, width)
    owned = (
        lax.psum_scatter(
            gain_one_grad.astype(jnp.bfloat16), "shard", scatter_dimension=0, tiled=True
        ).astype(jnp.float32),
        *tuple(
            (
                part.astype(jnp.float32)
                for part in sent_together(
                    (shift_one_grad.astype(jnp.bfloat16), qkv_w_grad.astype(jnp.bfloat16)),
                    "shard",
                    0,
                    1,
                )
            )
        ),
        lax.psum_scatter(
            qv_b_grad.astype(jnp.bfloat16), "shard", scatter_dimension=0, tiled=True
        ).astype(jnp.float32),
        *tuple(
            (
                part.astype(jnp.float32)
                for part in sent_together(
                    (
                        out_w_grad.astype(jnp.bfloat16),
                        out_b_grad.astype(jnp.bfloat16),
                        gain_two_grad.astype(jnp.bfloat16),
                        shift_two_grad.astype(jnp.bfloat16),
                        up_w_grad.astype(jnp.bfloat16),
                    ),
                    "shard",
                    0,
                    1,
                )
            )
        ),
        *tuple(
            (
                part.astype(jnp.float32)
                for part in sent_together(
                    (up_b_grad.astype(jnp.bfloat16), down_w_grad.astype(jnp.bfloat16)),
                    "shard",
                    0,
                    1,
                )
            )
        ),
        lax.psum_scatter(
            down_b_grad.astype(jnp.bfloat16), "shard", scatter_dimension=0, tiled=True
        ).astype(jnp.float32),
    )
    final = (
        lax.psum(owned[0].astype(jnp.bfloat16), "rep").astype(jnp.float32),
        lax.psum(owned[1].astype(jnp.bfloat16), "rep").astype(jnp.float32),
        lax.psum(owned[2].astype(jnp.bfloat16), "rep").astype(jnp.float32),
        lax.psum(owned[3].astype(jnp.bfloat16), "rep").astype(jnp.float32),
        lax.psum(owned[4].astype(jnp.bfloat16), "rep").astype(jnp.float32),
        lax.psum(owned[5].astype(jnp.bfloat16), "rep").astype(jnp.float32),
        lax.psum(owned[6].astype(jnp.bfloat16), "rep").astype(jnp.float32),
        lax.psum(owned[7].astype(jnp.bfloat16), "rep").astype(jnp.float32),
        lax.psum(owned[8].astype(jnp.bfloat16), "rep").astype(jnp.float32),
        lax.psum(owned[9].astype(jnp.bfloat16), "rep").astype(jnp.float32),
        lax.psum(owned[10].astype(jnp.bfloat16), "rep").astype(jnp.float32),
        lax.psum(owned[11].astype(jnp.bfloat16), "rep").astype(jnp.float32),
    )
    return (
        outputs,
        input_grad,
        final[0],
        final[1],
        final[2],
        final[3],
        final[4],
        final[5],
        final[6],
        final[7],
        final[8],
        final[9],
        final[10],
        final[11],
    )


def solution(mesh):
    placed = (
        P(("rep", "shard"), None, None),
        P(("rep", "shard"), None, None),
        P("shard"),
        P("shard"),
        P("shard", None),
        P("shard"),
        P("shard", None),
        P("shard"),
        P("shard"),
        P("shard"),
        P("shard", None),
        P("shard"),
        P("shard", None),
        P("shard"),
    )
    return jax.shard_map(
        local,
        mesh=mesh,
        in_specs=placed,
        out_specs=(
            P(("rep", "shard"), None, None),
            P(("rep", "shard"), None, None),
            P("shard"),
            P("shard"),
            P("shard", None),
            P("shard"),
            P("shard", None),
            P("shard"),
            P("shard"),
            P("shard"),
            P("shard", None),
            P("shard"),
            P("shard", None),
            P("shard"),
        ),
        check_vma=False,
    )
```

profile of v0, /device:TPU:2, one launch (start us, length us, event | category | flops | bytes accessed | tf_op | source)
XLA Modules:
  0.0 729.5 jit_solution(4068180039499892306)
XLA Ops:
  18.8 15.1 %all_gather.23 = bf16[384,1153]{1,0:T(8,128)(2,1)S(1)} all-gather(bf16[96,1153]{1,0:T(8,128)(2,1)S(1)} %pad_maximum_fusion.3), channel_id=1, replica_groups=mesh['rep'=32,'shard'=4] {'shard'}, dimensions={0}, use_global_device_ids=true | all-gather | bytes 1106880 | tf_op jit(solution)/shard_map/all_gather | solution.py:15
  36.5 10.4 %all-reduce.9 = (bf16[768]{0:T(1024)(128)(2,1)S(1)}, bf16[384]{0:T(512)(128)(2,1)S(1)}) all-reduce(bf16[768]{0:T(1024)(128)(2,1)S(1)} %dynamic-update-slice.1, bf16[384]{0:T(512)(128)(2,1)S(1)} %dynamic-update-slice), channel_id=1, replica_groups=mesh['rep'=32,'shard'=4] {'shard'}, use_global_device_ids=true, to_apply=%add.1 | all-reduce | flops 1152 | bytes 4608
  47.1 5.8 fusion.37
  56.2 6.6 reshape.321
  62.8 6.3 copy.83
  69.2 4.7 reshape.322
  73.8 6.4 copy.81
  80.3 4.7 reshape.323
  85.0 5.2 copy.82
  90.2 9.9 %multiply_reduce_fusion.1 = (f32[12,6,197]{2,1,0:T(8,128)S(1)}, f32[12,6,197,197]{2,3,1,0:T(8,128)}) fusion(bf16[12,197,6,64]{1,3,2,0:T(8,128)(2,1)} %copy.81, bf16[12,197,6,64]{1,3,2,0:T(8,128)(2,1)S(1)} %copy.82), kind=kOutput, calls=%fused_computation.32 | convolution fusion | flops 363238048 | bytes 14864832 | tf_op jit(solution)/shard_map/bqhe,bkhe->bhqk/dot_general | solution.py:96
  100.1 8.8 %fusion.13 = f32[12,6,197]{2,1,0:T(8,128)S(1)} fusion(f32[12,6,197,197]{2,3,1,0:T(8,128)} %get-tuple-element.101, f32[12,6,197]{2,1,0:T(8,128)S(1)} %get-tuple-element.100), kind=kLoop, calls=%fused_computation.31 | loop fusion | flops 8368560 | bytes 11290464 | tf_op jit(solution)/shard_map/reduce_sum | solution.py:101
  108.9 8.6 %convert_bitcast_fusion.1 = bf16[12,197,6,64]{1,3,2,0:T(8,128)(2,1)S(1)} fusion(bf16[12,197,6,64]{1,3,2,0:T(8,128)(2,1)S(1)} %copy-done.10, f32[12,6,197,197]{2,3,1,0:T(8,128)} %get-tuple-element.101, f32[12,6,197]{2,1,0:T(8,128)S(1)} %fusion.13, f32[12,6,197]{2,1,0:T(8,128)S(1)} %get-tuple-element.100), kind=kOutput, calls=%fused_computation.69 | convolution fusion | flops 369748512 | bytes 14921568 | tf_op jit(solution)/shard_map/bhqk,bkhe->bqhe/dot_general | solution.py:104
  135.9 38.9 %multiply_convert_fusion.1 = (bf16[2364,1536]{1,0:T(8,128)(2,1)}, f32[2364,1536]{1,0:T(8,128)}, f32[2364,1536]{1,0:T(8,128)}) fusion(f32[1536]{0:T(1024)S(1)} %convert_reduce_fusion.1, bf16[384,1923]{1,0:T(8,128)(2,1)S(1)} %copy-done.17, f32[2364,384]{1,0:T(8,128)S(1)} %get-tuple-element.103, f32[384]{0:T(512)S(1)} %get-tuple-element.63, ...), kind=kOutput, calls=%fused_computation.16 | convolution fusion | flops 3032879616 | bytes 41164800 | tf_op jit(solution)/shard_map/dot_general | solution.py:112
  174.8 17.6 %fusion.54 = (bf16[1536]{0:T(1024)(128)(2,1)S(1)}, bf16[2364,1536]{1,0:T(8,128)(2,1)}) fusion(f32[2364,1536]{1,0:T(8,128)} %get-tuple-element.93, f32[2364,1536]{1,0:T(8,128)} %get-tuple-element.104, bf16[2364,384]{1,0:T(8,128)(2,1)S(1)} %reshape.278, bf16[1536,385]{1,0:T(8,128)(2,1)} %all-gather.5.cloned.1.call-done), kind=kOutput, calls=%fused_computation.122 | convolution fusion | flops 2843152896 | bytes 39358464 | tf_op jit(solution)/shard_map/td,fd->tf/dot_general | solution.py:148
  192.4 9.5 %multiply_reduce_fusion.3 = (bf16[384]{0:T(512)(128)(2,1)}, f32[2364]{0:T(1024)S(1)}, bf16[384]{0:T(512)(128)(2,1)}, f32[2364,384]{1,0:T(8,128)S(1)}) fusion(f32[2364,384]{1,0:T(8,128)S(1)} %get-tuple-element.103, f32[2364]{0:T(1024)S(1)} %fusion.41, f32[2364]{0:T(1024)S(1)} %broadcast_multiply_fusion.1, f32[384]{0:T(512)S(1)} %get-tuple-element.62, ...), kind=kOutput, calls=%fused_computation.54 | convolution fusion | flops 2795947008 | bytes 15747824 | tf_op jit(solution)/shard_map/tf,df->td/dot_general | solution.py:153
  207.6 4.7 reshape.324
  212.3 5.1 copy.91
  217.3 11.8 %multiply_reduce_fusion = (f32[12,6,197]{2,1,0:T(8,128)S(1)}, f32[12,6,197,197]{2,3,1,0:T(8,128)}) fusion(f32[12,6,197,197]{2,3,1,0:T(8,128)} %get-tuple-element.101, f32[12,6,197]{2,1,0:T(8,128)S(1)} %copy-done.15, bf16[12,197,6,64]{1,3,2,0:T(8,128)(2,1)S(1)} %copy.91, bf16[12,197,6,64]{1,3,2,0:T(8,128)(2,1)} %copy.83), kind=kOutput, calls=%fused_computation.2 | convolution fusion | flops 368826528 | bytes 26098560 | tf_op jit(solution)/shard_map/bqhe,bkhe->bhqk/dot_general | solution.py:173
  229.2 10.9 %multiply_convert_fusion = bf16[12,6,197,197]{2,3,1,0:T(8,128)(2,1)S(1)} fusion(f32[12,6,197,197]{2,3,1,0:T(8,128)} %get-tuple-element.107, f32[12,6,197,197]{2,3,1,0:T(8,128)} %get-tuple-element.101, f32[12,6,197]{2,1,0:T(8,128)S(1)} %get-tuple-element.106, f32[12,6,197]{2,1,0:T(8,128)S(1)} %copy-done.15), kind=kLoop, calls=%fused_computation.1 | loop fusion | flops 13971240 | bytes 28055952 | tf_op jit(solution)/shard_map/convert_element_type | solution.py:177
  246.2 10.2 %fusion.52 = (bf16[6,64]{1,0:T(8,128)(2,1)}, bf16[12,197,6,64]{1,3,2,0:T(8,128)(2,1)}) fusion(bf16[12,197,6,64]{1,3,2,0:T(8,128)(2,1)S(1)} %copy.91, f32[12,6,197,197]{2,3,1,0:T(8,128)} %get-tuple-element.101, f32[12,6,197]{2,1,0:T(8,128)S(1)} %copy-done.15), kind=kOutput, calls=%fused_computation.120 | convolution fusion | flops 367861664 | bytes 14865600 | tf_op jit(solution)/shard_map/bhqk,bqhe->bkhe/dot_general | solution.py:170
  267.4 4.9 reshape.281
  286.1 10.3 %multiply_reduce_fusion.4 = (bf16[384]{0:T(512)(128)(2,1)}, f32[2364]{0:T(1024)}, bf16[384]{0:T(512)(128)(2,1)S(1)}, f32[2364,384]{1,0:T(8,128)}) fusion(f32[2364,384]{1,0:T(8,128)S(1)} %copy-done, f32[2364]{0:T(1024)S(1)} %copy-done.22, f32[2364]{0:T(1024)S(1)} %copy-done.20, f32[384]{0:T(512)S(1)} %copy-done.26, ...), kind=kOutput, calls=%fused_computation.55 | convolution fusion | flops 2098775040 | bytes 13637360 | tf_op jit(solution)/shard_map/te,de->td/dot_general | solution.py:203
  302.2 6.3 convolution_convert_fusion.1
  315.1 7.6 %convolution_convert_fusion.2 = bf16[384,1536]{1,0:T(8,128)(2,1)S(1)} fusion(bf16[2364,1536]{1,0:T(8,128)(2,1)} %get-tuple-element.114, f32[2364,384]{1,0:T(8,128)} %copy-done.2, f32[384]{0:T(512)} %copy-done.33, f32[384]{0:T(512)} %copy-done.30, f32[2364]{0:T(1024)S(1)} %fusion.41, f32[2364]{0:T(1024)S(1)} %broadcast_multiply_fusion.1), kind=kOutput, calls=%fused_computation.64 | convolution fusion | flops 2793816576 | bytes 12094944 | tf_op jit(solution)/shard_map/td,tf->df/dot_general | solution.py:151
  330.0 7.4 %all-reduce.8 = (bf16[384]{0:T(512)(128)(2,1)S(1)}, bf16[384]{0:T(512)(128)(2,1)S(1)}, bf16[768]{0:T(1024)(128)(2,1)S(1)}, bf16[384]{0:T(512)(128)(2,1)S(1)}) all-reduce(bf16[384]{0:T(512)(128)(2,1)S(1)} %dynamic-update-slice.2, bf16[384]{0:T(512)(128)(2,1)S(1)} %copy-done.37, ...), channel_id=1, replica_groups=mesh['rep'=32,'shard'=4] {'shard'}, use_global_device_ids=true, to_apply=%add.2 | all-reduce | flops 1920 | bytes 7680
  337.4 10.0 %fusion.22 = bf16[2364,384]{1,0:T(8,128)(2,1)} fusion(f32[2364,384]{1,0:T(8,128)} %copy-done.2, bf16[2364,1536]{1,0:T(8,128)(2,1)} %get-tuple-element.92, f32[384]{0:T(512)S(1)} %convert_element_type.274, bf16[1536,385]{1,0:T(8,128)(2,1)} %all-gather.5.cloned.1.call-done), kind=kOutput, calls=%fused_computation.46 | convolution fusion | flops 2791411200 | bytes 13908480 | tf_op jit(solution)/shard_map/dot_general | solution.py:118
  350.4 6.0 fusion.46
  358.1 13.1 %reduce-scatter.10.cloned.1.call-done = bf16[384,385]{1,0:T(8,128)(2,1)} async-done(((bf16[1536,385]{1,0:T(8,128)(2,1)}), bf16[384,385]{1,0:T(8,128)(2,1)}) %reduce-scatter.10.cloned.1.call-update) | async-done | bytes 295696
  373.3 35.0 %reduce-scatter.8.cloned.1.call-done = bf16[96,1923]{1,0:T(8,128)(2,1)} async-done(((bf16[384,1923]{1,0:T(8,128)(2,1)}), bf16[96,1923]{1,0:T(8,128)(2,1)}) %reduce-scatter.8.cloned.1.call-update) | async-done | bytes 369232 | tf_op jit(solution)/shard_map/reduce_scatter | solution.py:26
  411.6 4.8 add_convert_fusion
  422.5 80.5 %all-reduce.6 = (bf16[96]{0:T(256)(128)(2,1)S(1)}, bf16[96]{0:T(256)(128)(2,1)S(1)}, bf16[192]{0:T(256)(128)(2,1)S(1)}, bf16[96]{0:T(256)(128)(2,1)S(1)}, bf16[9...) all-reduce(bf16[96]{0:T(256)(128)(2,1)S(1)} %dynamic-slice.4, ...), channel_id=1, replica_groups=mesh['rep'=32,'shard'=4] {'rep'}, use_global_device_ids=true, to_apply=%region_13.0 | all-reduce | flops 1152 | bytes 4608 | tf_op jit(solution)/shard_map/psum | solution.py:262
  507.2 208.2 %all-reduce.12.cloned.1.call-done = (bf16[384,384]{0,1:T(8,128)(2,1)}, bf16[96,1152]{1,0:T(8,128)(2,1)}, bf16[96,384]{1,0:T(8,128)(2,1)}, bf16[96,1536]{1,0:T(8,128)(2,1)}) async-done(((bf16[384,384]{0,1:T(8,128)(2,1)}, bf16[96,1152]{1,0:T(8,128)(2,1)}, bf16[96,384]{1,0:T(8,128)(2,1)}, bf16[96,1536]{1,0:T(8,128)(2,1)}), (bf16[384,384]{0,1:T(8,128)(2,1)}, bf16[96,1152]{1,0:T(8,128)(2,1)}, ...) | async-done | bytes 884752 | tf_op jit(solution)/shard_map/psum | solution.py:272
  (196 shorter events, 116.8 us)
Async XLA Ops:
  7.2 7.4 %copy-start.6 = (bf16[12,197,384]{2,1,0:T(8,128)(2,1)S(1)}, bf16[12,197,384]{2,1,0:T(8,128)(2,1)}, u32[]{:S(2)}) copy-start(bf16[12,197,384]{2,1,0:T(8,128)(2,1)} %param.14) | copy-start | bytes 5446660
  7.2 119.4 %all-gather.5.cloned.1.call-start = ((), (), s32[]{:S(2)}) async-start(), calls=%async_computation.4 | async-start | bytes 1966080 | tf_op jit(solution)/shard_map/all_gather | solution.py:15
  10.1 117.7 %all-gather.3.cloned.1.call-start = ((), (), s32[]{:S(2)}) async-start(), calls=%async_computation.3 | async-start | bytes 1966080 | tf_op jit(solution)/shard_map/all_gather | solution.py:15
  14.5 341.8 %reduce-scatter.6.cloned.1.call-start = ((), (), s32[]{:S(2)}) async-start(), calls=%async_computation.5 | async-start | bytes 1228800 | tf_op jit(solution)/shard_map/reduce_scatter | solution.py:26
  16.8 17.2 %copy-start.34 = (u32[128]{0:T(128)S(1)}, u32[128]{0:T(128)}, u32[]{:S(2)}) copy-start(u32[128]{0:T(128)} %constant.92) | copy-start | bytes 1540
  16.8 19.2 %copy-start.39 = (bf16[192]{0:T(256)(128)(2,1)S(1)}, bf16[192]{0:T(256)(128)(2,1)}, u32[]{:S(2)}) copy-start(bf16[192]{0:T(256)(128)(2,1)} %param.19) | copy-start | bytes 1156
  16.8 19.5 %copy-start.40 = (bf16[96]{0:T(256)(128)(2,1)S(1)}, bf16[96]{0:T(256)(128)(2,1)}, u32[]{:S(2)}) copy-start(bf16[96]{0:T(256)(128)(2,1)} %param.16) | copy-start | bytes 580
  18.5 34.4 %copy-start.19 = (f32[2364]{0:T(1024)}, f32[2364]{0:T(1024)S(1)}, u32[]{:S(2)}) copy-start(f32[2364]{0:T(1024)S(1)} %div.51) | copy-start | bytes 28372
  33.9 19.0 %copy-start.13 = (bf16[384,1153]{1,0:T(8,128)(2,1)}, bf16[384,1153]{1,0:T(8,128)(2,1)S(1)}, u32[]{:S(2)}) copy-start(bf16[384,1153]{1,0:T(8,128)(2,1)S(1)} %all_gather.23) | copy-start | bytes 2656516
  34.0 18.9 %copy-start.27 = (f32[384]{0:T(512)}, f32[384]{0:T(512)S(1)}, u32[]{:S(2)}) copy-start(f32[384]{0:T(512)S(1)} %convert_reduce_fusion.5) | copy-start | bytes 4612
  46.9 6.0 copy-start.25
  73.8 6.4 copy-start.12
  90.1 9.9 %copy-start.3 = (bf16[12,197,6,64]{1,3,2,0:T(8,128)(2,1)}, bf16[12,197,6,64]{1,3,2,0:T(8,128)(2,1)S(1)}, u32[]{:S(2)}) copy-start(bf16[12,197,6,64]{1,3,2,0:T(8,128)(2,1)S(1)} %copy.82) | copy-start | bytes 5446660
  100.1 8.8 %copy-start.10 = (bf16[12,197,6,64]{1,3,2,0:T(8,128)(2,1)S(1)}, bf16[12,197,6,64]{1,3,2,0:T(8,128)(2,1)}, u32[]{:S(2)}) copy-start(bf16[12,197,6,64]{1,3,2,0:T(8,128)(2,1)} %copy.83) | copy-start | bytes 5446660
  125.8 77.5 %copy-start.7 = (bf16[2364,384]{1,0:T(8,128)(2,1)}, bf16[2364,384]{1,0:T(8,128)(2,1)S(1)}, u32[]{:S(2)}) copy-start(bf16[2364,384]{1,0:T(8,128)(2,1)S(1)} %reshape.278) | copy-start | bytes 5446660
  129.1 72.7 %copy-start.30 = (f32[384]{0:T(512)}, f32[384]{0:T(512)S(1)}, u32[]{:S(2)}) copy-start(f32[384]{0:T(512)S(1)} %get-tuple-element.62) | copy-start | bytes 4612
  133.4 68.5 %copy-start.2 = (f32[2364,384]{1,0:T(8,128)}, f32[2364,384]{1,0:T(8,128)S(1)}, u32[]{:S(2)}) copy-start(f32[2364,384]{1,0:T(8,128)S(1)} %get-tuple-element.103) | copy-start | bytes 10893316
  229.2 10.9 %copy-start.4 = (bf16[12,197,6,64]{1,3,2,0:T(8,128)(2,1)S(1)}, bf16[12,197,6,64]{1,3,2,0:T(8,128)(2,1)}, u32[]{:S(2)}) copy-start(bf16[12,197,6,64]{1,3,2,0:T(8,128)(2,1)} %copy-done.3) | copy-start | bytes 5446660
  280.1 6.0 copy-start
  280.1 6.0 copy-start.14
  280.1 6.0 copy-start.20
  280.1 6.0 copy-start.22
  280.1 6.0 copy-start.26
  286.1 10.3 %copy-start.16 = (bf16[2364,1152]{0,1:T(8,128)(2,1)S(1)}, bf16[2364,1152]{0,1:T(8,128)(2,1)}, u32[]{:S(2)}) copy-start(bf16[2364,1152]{0,1:T(8,128)(2,1)} %constant_dynamic-update-slice_fusion) | copy-start | bytes 16339972
  286.1 10.3 %copy-start.28 = (f32[384]{0:T(512)S(1)}, f32[384]{0:T(512)}, u32[]{:S(2)}) copy-start(f32[384]{0:T(512)} %copy-done.27) | copy-start | bytes 4612
  301.7 69.5 %reduce-scatter.10.cloned.1.call-start = ((), (), s32[]{:S(2)}) async-start(), calls=%async_computation.7 | async-start | bytes 1966080
  310.4 97.9 %reduce-scatter.8.cloned.1.call-start = ((), (), s32[]{:S(2)}) async-start(), calls=%async_computation.6 | async-start | bytes 1966080 | tf_op jit(solution)/shard_map/reduce_scatter | solution.py:26
  322.7 6.8 copy-start.41
  322.7 7.1 copy-start.31
  322.7 7.2 copy-start.32
  322.7 7.3 copy-start.37
  326.3 389.1 %all-reduce.12.cloned.1.call-start = ((), (), s32[]{:S(2)}) async-start(), calls=%async_computation.8 | async-start | bytes 1769472 | tf_op jit(solution)/shard_map/psum | solution.py:272
  (16 other events, 60.4 us)
Sparse Core Ops, SparseCore 0:
  10.3 28.2 all-gather.4
  40.8 24.9 all-gather.2
  301.8 32.0 reduce-scatter.5
  336.6 34.5 reduce-scatter.9
  373.7 34.4 reduce-scatter.7
  412.2 303.1 all-reduce.11
where the time goes:
time: 735 us; the launch traced here: 730 us
  waiting for transfers between devices  256 us (35%)
  matrix products  165 us (22%)
  local copies, waits for them, and re-layouts  121 us (16%)
  blocking collectives  113 us (15%)
  other arithmetic  55.1 us (7%)
  between operations  17.7 us (2%)
    psum x1, waiting for transfers between devices, local(): lax.psum(owned[10].astype(jnp.bfloat16), 'rep').astype(jnp.float32)  208 us
    psum x1, blocking collectives, local(): lax.psum(owned[0].astype(jnp.bfloat16), 'rep').astype(jnp.float32)  80.5 us
    reshape x8, local copies, waits for them, and re-layouts, heads_view(): return tensor.reshape(images, length, HEADS, HEAD_DIM)  43.6 us
    dot_general x1, matrix products, local(): jnp.dot(normed_two, upw_full, preferred_element_type=jnp.float32)  38.9 us
    reduce_scatter x2, waiting for transfers between devices, sent_together(): lax.psum_scatter(both, axis, scatter_dimension=dim, tiled=True)  35 us
    unnamed x2, blocking collectives  17.8 us
    dot_general x1, matrix products, local(): jnp.einsum('td,fd->tf', cotangent, downw_back, preferred_element_type=jnp...  17.6 us
    unnamed x99, local copies, waits for them, and re-layouts  16.3 us
  transfers between devices with their start and end apart: 6, of which 3 were waited for; matrix products, arithmetic and copies ran while one was open for 21% of the time, Pallas kernels for 0%

commit v1 on v0

v1 whole, which is shorter than its diff:
```python
import math

import jax
import jax.numpy as jnp
from jax import lax
from jax.experimental import pallas as pl
from jax.experimental.pallas import tpu as pltpu
from jax.sharding import PartitionSpec as P

NI, SEQ, D, FF, HEADS = 12, 197, 384, 1536, 6
PAD = 208
ROWS = NI * PAD
TROWS = 2560
F32, BF16 = jnp.float32, jnp.bfloat16


def mm(a, b):
    return lax.dot_general(a, b, (((1,), (0,)), ((), ())), preferred_element_type=F32)


def mm_nt(a, b):
    return lax.dot_general(a, b, (((1,), (1,)), ((), ())), preferred_element_type=F32)


def mm_tn(a, b):
    return lax.dot_general(a, b, (((0,), (0,)), ((), ())), preferred_element_type=F32)


def norm_parts(v):
    avg = jnp.mean(v, axis=-1, keepdims=True)
    cen = v - avg
    var = jnp.mean(cen * cen, axis=-1, keepdims=True)
    rs = lax.rsqrt(var + 1e-6)
    return cen * rs, rs


def norm_back(e, n, rs):
    return rs * (e - jnp.mean(e, axis=-1, keepdims=True) - n * jnp.mean(e * n, axis=-1, keepdims=True))


def gelu_both(u):
    a = jnp.abs(u)
    d = 1.0 + (0.3275911 * math.sqrt(0.5)) * a
    t = 1.0 / d
    e = jnp.exp2(u * u * (-0.5 * math.log2(math.e)))
    p = (0.5 * 1.061405429) * t - (0.5 * 1.453152027)
    p = p * t + (0.5 * 1.421413741)
    p = p * t - (0.5 * 0.284496736)
    p = p * t + (0.5 * 0.254829592)
    tail = p * t * e
    phi = jnp.where(u < 0, tail, 1.0 - tail)
    return u * phi, phi + u * (e * (1.0 / math.sqrt(2 * math.pi)))


def colsum(v):
    return jnp.sum(v, axis=0, keepdims=True)

CH1, CH2, CH4 = 2, 2, 2
MESH = pl.DeviceIdType.MESH

UP_ROW, DOWN_ROW, OUT_ROW, QKV_ROW = 0, 1152, 2304, 2592
GROWS = 3584
GROUPS = ((0, 160), (2560, 32), (3072, 32))


class Comm:
    def __init__(self, ssem, rsem):
        self.ssem, self.rsem = ssem, rsem
        rep, shard = lax.axis_index("rep"), lax.axis_index("shard")
        self.z, self.y, self.lo = rep // 8, (rep // 2) % 4, rep % 2
        self.hi, self.core, self.plane = shard // 2, shard % 2, rep // 2
        self.sibling = (rep, self.hi * 2 + 1 - self.core)
        self.across = (self.plane * 2 + 1 - self.lo, (1 - self.hi) * 2 + self.core)
        self.row = []
        for dh, dl in ((0, 1), (1, 0), (1, 1)):
            ph, plo = (self.hi + dh) % 2, (self.lo + dl) % 2
            self.row.append(((self.plane * 2 + plo, ph * 2 + self.core), ph))
        self.planes = []
        for d in range(1, 16):
            pz, py = (self.z + d // 4) % 4, (self.y + d % 4) % 4
            q = pz * 4 + py
            self.planes.append(((q * 2 + self.lo, shard), q))

    def barrier(self):
        sem = pltpu.get_barrier_semaphore()
        peers = [self.sibling] + [d for d, _ in self.row] + [d for d, _ in self.planes]
        for dev in peers:
            pl.semaphore_signal(sem, inc=1, device_id=dev, device_id_type=MESH)
        pl.semaphore_wait(sem, len(peers))

    def copy(self, src, dst, slot, dev):
        return pltpu.make_async_remote_copy(
            src_ref=src, dst_ref=dst, send_sem=self.ssem.at[slot], recv_sem=self.rsem.at[slot],
            device_id=dev, device_id_type=MESH,
        )


class Reduce:
    def __init__(self, comm, base, grads, fin, start, n, rcore, rplane, part, rrow, scatter=True):
        c = comm
        self.c, self.n, self.scatter, self.start = c, n, scatter, start
        total = 16 * n if scatter else n
        self.grads, self.rcore, self.rplane, self.part, self.rrow, self.fin = (
            grads, rcore, rplane, part, rrow, fin)
        self.total = total
        rows = pl.ds(start, total)
        self.rows = rows
        self.core_copy = c.copy(grads.at[1 - c.core, :, rows, :], rcore, base, c.sibling)

        def piece(q):
            return pl.ds(pl.multiple_of(start + q * n, 16), n) if scatter else rows

        self.piece = piece
        self.plane_copies = [
            c.copy(grads.at[c.core, :, piece(q), :], rplane.at[d], base + 1 + d, dev)
            for d, (dev, q) in enumerate(c.planes)
        ]
        self.row_copies = [
            c.copy(part.at[h], rrow.at[d], base + 16 + d, dev)
            for d, (dev, h) in enumerate(c.row)
        ]
        if scatter:
            mine = piece(c.plane)
            self.back_copies = [
                c.copy(fin.at[mine, :], fin.at[mine, :], base + 19 + d, dev)
                for d, (dev, q) in enumerate(c.planes)
            ]

    def send_core(self):
        self.core_copy.start()

    def send_planes(self):
        self.core_copy.wait()
        step = 256 if self.total % 256 == 0 else 16

        @pl.loop(0, self.total // step)
        def _(b):
            off = pl.multiple_of(b * step, 16)
            r = pl.ds(pl.multiple_of(self.start + off, 16), step)
            for h in range(2):
                s = self.grads[self.c.core, h, r, :].astype(F32) + self.rcore[h, pl.ds(off, step), :].astype(F32)
                self.grads[self.c.core, h, r, :] = s.astype(BF16)

        for cp in self.plane_copies:
            cp.start()

    def send_row(self):
        for cp in self.plane_copies:
            cp.wait()
        for h in range(2):
            s = self.grads[self.c.core, h, self.piece(self.c.plane), :].astype(F32)
            for d in range(15):
                s = s + self.rplane[d, h].astype(F32)
            self.part[h] = s.astype(BF16)
        for cp in self.row_copies:
            cp.start()

    def send_back(self):
        for cp in self.row_copies:
            cp.wait()
        s = self.part[self.c.hi].astype(F32)
        for d in range(3):
            s = s + self.rrow[d].astype(F32)
        if self.scatter:
            self.fin[self.piece(self.c.plane), :] = s.astype(BF16)
            for cp in self.back_copies:
                cp.start()
        else:
            self.fin[...] = s.astype(BF16)

    def finish(self):
        for cp in self.back_copies:
            cp.wait()


def padded(ref, i, tmp):
    tmp[0:SEQ, :] = ref[i].astype(F32)
    return tmp[...]


def body(x_ref, dy_ref, vin_ref, wqkv_in, wo_in, wup_in, wd_in,
         out_ref, ig_ref, fin_ref, finv_ref,
         stage, out_sem, tmp, dys, dyT, tT, h1s, qkv, ps, cs, h2s, gs, dus, dbs,
         vecs_all, wqkv, wo, wup, wd, vec_ref, gvec, grads, gradv,
         rcore0, rplane0, part0, rrow0, rcore1, rplane1, part1, rrow1,
         rcore2, rplane2, part2, rrow2, rcorev, rplanev, partv, rrowv, fin, finv, ssem, rsem):
    dy_copy = pltpu.make_async_copy(dy_ref, stage, out_sem)
    dy_copy.start()
    comm = Comm(ssem, rsem)
    shard = comm.hi * 2 + comm.core
    theirs = (1 - comm.hi) * 2 + comm.core

    def place(full, s):
        n = full.shape[0] // 4
        return full.at[pl.ds(pl.multiple_of(s * n, 16), n)]

    params = ((wqkv_in, wqkv), (vin_ref, vecs_all), (wo_in, wo), (wup_in, wup), (wd_in, wd))
    for own, full in params:
        n = own.shape[0]
        full[pl.ds(pl.multiple_of(shard * n, 16), n), :] = own[...]
    comm.barrier()
    first, second, third = [], [], []
    for j, (own, full) in enumerate(params):
        first.append(comm.copy(own, place(full, shard), 3 * j, comm.across))
        second.append(comm.copy(own, place(full, shard), 3 * j + 1, comm.sibling))
        third.append(comm.copy(place(full, theirs), place(full, theirs), 3 * j + 2, comm.sibling))
        first[j].start()
        second[j].start()

    def forward(j):
        first[j].wait_recv()
        third[j].start()

    def gathered(j):
        second[j].wait_recv()
        third[j].wait_recv()

    red = [Reduce(comm, 16 + 40 * g, grads, fin, start, n, *bufs)
           for g, ((start, n), bufs) in enumerate(zip(GROUPS, (
               (rcore0, rplane0, part0, rrow0), (rcore1, rplane1, part1, rrow1),
               (rcore2, rplane2, part2, rrow2))))]
    redv = Reduce(comm, 136, gradv, finv, 0, 16, rcorev, rplanev, partv, rrowv, scatter=False)

    def vec(r):
        return vec_ref[r:r + 1, :]

    def vcat(r, n):
        return jnp.concatenate([vec_ref[r + j:r + j + 1, :] for j in range(n)], axis=1)

    tmp[...] = jnp.zeros_like(tmp)
    gvec[...] = jnp.zeros_like(gvec)
    for s in (dys, h1s, cs, h2s, gs, dus, dbs, qkv):
        s[ROWS:TROWS, :] = jnp.zeros((TROWS - ROWS, s.shape[1]), s.dtype)
    grads[:, :, QKV_ROW + 864:, :] = jnp.zeros((2, 2, GROWS - QKV_ROW - 864, 128), BF16)
    dy_copy.wait()

    @pl.loop(0, NI)
    def _(i):
        r = pl.ds(pl.multiple_of(i * PAD, 16), PAD)
        dy = padded(stage, i, tmp)
        dys[r, :] = dy.astype(BF16)
        gvec[5:6, :] += colsum(dy)

    forward(0)
    forward(1)
    gathered(1)
    vec_ref[...] = (
        vecs_all[0:16, :].astype(F32) + vecs_all[16:32, :].astype(F32)
        + vecs_all[32:48, :].astype(F32) + vecs_all[48:64, :].astype(F32)
    )

    @pl.loop(0, NI)
    def _(i):
        r = pl.ds(pl.multiple_of(i * PAD, 16), PAD)
        n, _ = norm_parts(padded(x_ref, i, tmp))
        h1s[r, :] = (n * vec(0) + vec(1)).astype(BF16)

    def transpose_into(dst, src):
        @pl.loop(0, TROWS // 256)
        def _(b):
            r = pl.ds(pl.multiple_of(b * 256, 256), 256)
            dst[:, r] = src[r, :].T

    transpose_into(dyT, dys)
    gathered(0)

    lane = lax.broadcasted_iota(jnp.int32, (1, 128), 1)
    halves = (lane < 64, lane >= 64)
    keycol = lax.broadcasted_iota(jnp.int32, (1, PAD), 1) < SEQ
    zero = jnp.zeros((), BF16)

    def half(v, h):
        return jnp.where(halves[h], v, zero)

    @pl.loop(0, NI // CH1)
    def _(c):
        r = pl.ds(pl.multiple_of(c * (CH1 * PAD), 16), CH1 * PAD)
        p = mm(h1s[r, :], wqkv[...]) + vcat(6, 3)
        qkv[r, 0:D] = (p[:, 0:D] * 0.125).astype(BF16)
        qkv[r, D:3 * D] = p[:, D:].astype(BF16)

    def attention(first_image, last_image):
        @pl.loop(first_image, last_image)
        def _(i):
            r = pl.ds(pl.multiple_of(i * PAD, 16), PAD)
            for p in range(3):
                q = qkv[r, 128 * p:128 * p + 128]
                k = qkv[r, D + 128 * p:D + 128 * p + 128]
                v = qkv[r, 2 * D + 128 * p:2 * D + 128 * p + 128]
                acc = None
                for h in range(2):
                    s = mm_nt(q, half(k, h))
                    s = jnp.where(keycol, s, -1e30)
                    e = jnp.exp(s - jnp.max(s, axis=-1, keepdims=True))
                    pr = (e * (1.0 / jnp.sum(e, axis=-1, keepdims=True))).astype(BF16)
                    ps[i * HEADS + 2 * p + h] = pr
                    o = mm(pr, half(v, h))
                    acc = o if acc is None else acc + o
                cs[r, 128 * p:128 * p + 128] = acc.astype(BF16)

    attention(0, 6)
    forward(2)
    attention(6, 12)
    forward(3)
    forward(4)
    for j in (2, 3, 4):
        gathered(j)

    @pl.loop(0, NI // CH2)
    def _(c):
        r = pl.ds(pl.multiple_of(c * (CH2 * PAD), 16), CH2 * PAD)
        xs = jnp.concatenate([padded(x_ref, c * CH2 + j, tmp) for j in range(CH2)], axis=0)
        x1 = xs + mm(cs[r, :], wo[...]) + vec(2)
        n2, rs2 = norm_parts(x1)
        h2 = (n2 * vec(3) + vec(4)).astype(BF16)
        h2s[r, :] = h2
        dy = dys[r, :]
        acc, dh = x1 + vec(5), None
        for f in range(4):
            fc = slice(f * D, f * D + D)
            u = mm(h2, wup[:, fc]) + vec(9 + f)
            g, gp = gelu_both(u)
            g = g.astype(BF16)
            gs[r, fc] = g
            acc = acc + mm(g, wd[fc, :])
            du = (mm_nt(dy, wd[fc, :]) * gp).astype(BF16)
            dus[r, fc] = du
            gvec[9 + f:10 + f, :] += colsum(du.astype(F32))
            o = mm_nt(du, wup[:, fc])
            dh = o if dh is None else dh + o
        for j in range(CH2):
            stage[c * CH2 + j] = acc[j * PAD:j * PAD + SEQ].astype(BF16)
        gvec[3:4, :] += colsum(dh * n2)
        gvec[4:5, :] += colsum(dh)
        dx1 = dy.astype(F32) + norm_back(dh * vec(3), n2, rs2)
        db = dx1.astype(BF16)
        dbs[r, :] = db
        gvec[2:3, :] += colsum(db.astype(F32))
        dys[r, :] = mm_nt(db, wo[...]).astype(BF16)

    out_copy = pltpu.make_async_copy(stage, out_ref, out_sem)
    out_copy.start()

    def put(value, row):
        value = value.astype(BF16)
        for s in range(4):
            for b in range(value.shape[1] // 128):
                r = pl.ds(pl.multiple_of(row + 96 * b, 16), 96)
                grads[s % 2, s // 2, r, :] = value[96 * s:96 * s + 96, 128 * b:128 * b + 128]

    @pl.loop(0, 2)
    def _(h):
        for core in range(2):
            cc = pl.ds(pl.multiple_of(h * 768 + core * 384, 128), 384)
            value = mm(dyT[...], gs[:, cc]).astype(BF16)
            for b in range(3):
                grads[core, h, DOWN_ROW + 384 * b:DOWN_ROW + 384 * b + 384, :] = value[:, 128 * b:128 * b + 128]

    transpose_into(tT, h2s)

    @pl.loop(0, 4)
    def _(n):
        cc = pl.ds(pl.multiple_of(n * 384, 128), 384)
        put(mm(tT[...], dus[:, cc]), UP_ROW + 288 * n)

    transpose_into(tT, cs)
    put(mm(tT[...], dbs[...]), OUT_ROW)
    red[0].send_core()
    transpose_into(tT, h1s)

    def attention_back(p):
        sl = [slice(j * D + 128 * p, j * D + 128 * p + 128) for j in range(3)]

        @pl.loop(0, NI)
        def _(i):
            r = pl.ds(pl.multiple_of(i * PAD, 16), PAD)
            q, k, v = (qkv[r, s] for s in sl)
            dc = dys[r, 128 * p:128 * p + 128]
            dq = dk = dv = None
            for h in range(2):
                pr = ps[i * HEADS + 2 * p + h]
                da = mm_nt(dc, half(v, h))
                prf = pr.astype(F32)
                t = prf * da
                ds = (t - prf * jnp.sum(t, axis=-1, keepdims=True)).astype(BF16)
                ov = mm_tn(pr, half(dc, h))
                oq = mm(ds, half(k, h))
                ok = mm_tn(ds, half(q, h))
                if dq is None:
                    dq, dk, dv = oq, ok, ov
                else:
                    dq, dk, dv = dq + oq, dk + ok, dv + ov
            for j, o in enumerate((dq * 0.125, dk, dv)):
                o = o.astype(BF16)
                qkv[r, sl[j]] = o
                if j != 1:
                    gvec[6 + j:7 + j, 128 * p:128 * p + 128] += colsum(o.astype(F32))

    def qkv_grad(p):
        rhs = jnp.concatenate([qkv[:, j * D + 128 * p:j * D + 128 * p + 128] for j in range(3)], axis=1)
        put(mm(tT[...], rhs), QKV_ROW + 288 * p)

    attention_back(0)
    red[0].send_planes()
    qkv_grad(0)
    attention_back(1)
    red[0].send_row()
    qkv_grad(1)
    red[1].send_core()
    attention_back(2)
    red[0].send_back()
    red[1].send_planes()
    qkv_grad(2)
    red[2].send_core()
    out_copy.wait()

    def first_norm_back(a, b):
        @pl.loop(a // CH4, b // CH4)
        def _(c):
            r = pl.ds(pl.multiple_of(c * (CH4 * PAD), 16), CH4 * PAD)
            dh = mm_nt(qkv[r, :], wqkv[...])
            xs = jnp.concatenate([padded(x_ref, c * CH4 + j, tmp) for j in range(CH4)], axis=0)
            n1, rs1 = norm_parts(xs)
            gvec[0:1, :] += colsum(dh * n1)
            gvec[1:2, :] += colsum(dh)
            ig = dbs[r, :].astype(F32) + norm_back(dh * vec(0), n1, rs1)
            for j in range(CH4):
                stage[c * CH4 + j] = ig[j * PAD:j * PAD + SEQ].astype(BF16)

    first_norm_back(0, 4)
    red[2].send_planes()
    first_norm_back(4, 8)
    red[1].send_row()
    first_norm_back(8, 12)

    ig_copy = pltpu.make_async_copy(stage, ig_ref, out_sem)
    ig_copy.start()
    gv = gvec[...]
    for s in range(4):
        moved = gv if s == 0 else pltpu.roll(gv, D - 96 * s, 1)
        bias = gv if s % 2 == 0 else pltpu.roll(gv, D - 192, 1)
        br = 6 if s < 2 else 8
        tile = jnp.concatenate(
            [moved[0:6, 0:128], bias[br:br + 1, 0:128], bias[br:br + 1, 128:256]]
            + [gv[9 + s:10 + s, 128 * b:128 * b + 128] for b in range(3)] + [jnp.zeros((5, 128), F32)],
            axis=0,
        )
        gradv[s % 2, s // 2] = tile.astype(BF16)
    redv.send_core()
    red[2].send_row()
    redv.send_planes()
    red[1].send_back()
    red[2].send_back()
    redv.send_row()
    for g in (0, 1, 2):
        red[g].finish()
    redv.send_back()
    fin_ref[...] = fin[...]
    finv_ref[...] = finv[...]
    for j in range(5):
        first[j].wait_send()
        second[j].wait_send()
        third[j].wait_send()
    ig_copy.wait()


def scratches():
    V = pltpu.VMEM
    bufs = []
    for n, full in ((160, 2560), (32, 512), (32, 512), (16, 16)):
        bufs += [V((2, full, 128), BF16), V((15, 2, n, 128), BF16), V((2, n, 128), BF16), V((3, n, 128), BF16)]
    return [
        V((NI, SEQ, D), BF16), pltpu.SemaphoreType.DMA,
        V((PAD, D), F32), V((TROWS, D), BF16), V((D, TROWS), BF16), V((D, TROWS), BF16),
        V((TROWS, D), BF16), V((TROWS, 3 * D), BF16), V((NI * HEADS, PAD, PAD), BF16),
        V((TROWS, D), BF16), V((TROWS, D), BF16), V((TROWS, FF), BF16), V((TROWS, FF), BF16),
        V((TROWS, D), BF16),
        V((64, D), BF16), V((D, 3 * D), BF16), V((D, D), BF16), V((D, FF), BF16), V((FF, D), BF16),
        V((16, D), F32), V((16, D), F32), V((2, 2, GROWS, 128), BF16), V((2, 2, 16, 128), BF16),
        *bufs,
        V((GROWS, 128), BF16), V((16, 128), BF16),
        pltpu.SemaphoreType.DMA((160,)), pltpu.SemaphoreType.DMA((160,)),
    ]


def layer(x, dy, vecs, wqkv, wo, wup, wd):
    S = jax.ShapeDtypeStruct
    vm, hbm = pl.BlockSpec(memory_space=pltpu.VMEM), pl.BlockSpec(memory_space=pl.ANY)
    return pl.pallas_call(
        body,
        out_shape=(S(x.shape, BF16), S(x.shape, BF16), S((GROWS, 128), BF16), S((16, 128), BF16)),
        in_specs=[vm, hbm] + [vm] * 5, out_specs=(hbm, hbm, vm, vm),
        scratch_shapes=scratches(),
        compiler_params=pltpu.CompilerParams(
            vmem_limit_bytes=int(63.5 * 2**20), collective_id=0, has_side_effects=True),
    )(x, dy, vecs, wqkv, wo, wup, wd)


def unpack_body(fin, finv, g1, s1, gqkv, gqv, go, bo, g2, s2, gup, bup, gd, bd):
    for b in range(12):
        gup[:, 128 * b:128 * b + 128] = fin[UP_ROW + 96 * b:UP_ROW + 96 * b + 96, :].astype(F32)
    for b in range(3):
        gd[128 * b:128 * b + 128, :] = fin[DOWN_ROW + 384 * b:DOWN_ROW + 384 * b + 384, :].astype(F32).T
        go[:, 128 * b:128 * b + 128] = fin[OUT_ROW + 96 * b:OUT_ROW + 96 * b + 96, :].astype(F32)
    for p in range(3):
        for j in range(3):
            r = QKV_ROW + 288 * p + 96 * j
            gqkv[:, j * D + 128 * p:j * D + 128 * p + 128] = fin[r:r + 96, :].astype(F32)
    v = finv[...].astype(F32)
    for row, ref in enumerate((g1, s1, bo, g2, s2, bd)):
        ref[...] = v[row, 0:96]
    gqv[0:128] = v[6, :]
    gqv[128:192] = v[7, 0:64]
    for b in range(3):
        bup[128 * b:128 * b + 128] = v[8 + b, :]


def unpack(fin, finv):
    def S(*shape):
        return jax.ShapeDtypeStruct(shape, F32)

    vm = pl.BlockSpec(memory_space=pltpu.VMEM)
    return pl.pallas_call(
        unpack_body,
        out_shape=(S(96), S(96), S(96, 3 * D), S(192), S(96, D), S(96), S(96), S(96),
                   S(96, FF), S(384), S(384, D), S(96)),
        in_specs=[vm] * 2, out_specs=(vm,) * 12,
        compiler_params=pltpu.CompilerParams(vmem_limit_bytes=24 * 2**20),
    )(fin, finv)


def local(inputs, out_grad, ln1_gain, ln1_shift, qkv_weight, qv_bias, out_weight, out_bias,
          ln2_gain, ln2_shift, up_weight, up_bias, down_weight, down_bias):
    shard = lax.axis_index("shard")
    lane = jnp.arange(D)
    six = jnp.stack([ln1_gain, ln1_shift, out_bias, ln2_gain, ln2_shift, down_bias])
    six = jnp.where(lane // 96 == shard, jnp.tile(six, (1, 4)), 0)
    two = jnp.where(lane // 192 == shard % 2, jnp.tile(qv_bias, 2), 0)
    row = jnp.arange(16)[:, None]
    vecs = jnp.concatenate([six, jnp.zeros((10, D), BF16)])
    vecs = jnp.where(row == 6 + 2 * (shard // 2), two, vecs)
    vecs = jnp.where(row == 9 + shard, up_bias, vecs)
    outputs, input_grad, fin, finv = layer(
        inputs, out_grad, vecs, qkv_weight, out_weight, up_weight, down_weight)
    return (outputs, input_grad, *unpack(fin, finv))


def solution(mesh):
    tokens, whole, rows = P(("rep", "shard"), None, None), P("shard"), P("shard", None)
    vectors = (whole, whole, rows, whole, rows, whole, whole, whole, rows, whole, rows, whole)
    return jax.shard_map(
        local, mesh=mesh, in_specs=(tokens, tokens, *vectors),
        out_specs=(tokens, tokens, *vectors), check_vma=False)
```

time: 735 us -> 171 us (0.23)
  waiting for transfers between devices: 256 us -> 0 us
  matrix products: 165 us -> 0 us
  Pallas kernels: 0 us -> 160 us
  local copies, waits for them, and re-layouts: 121 us -> 7.74 us
  blocking collectives: 113 us -> 0 us
  other arithmetic: 55.1 us -> 1.4 us
  between operations: 17.7 us -> 0.7 us
    psum x1 -> x0, waiting for transfers between devices: 208 us -> none  [local(): lax.psum(owned[10].astype(jnp.bfloat16), 'rep').astype(jnp.float32)]
    dot_general x18 -> x0, matrix products: 165 us -> none  [the longest x1 38.9 us: local(): jnp.dot(normed_two, upw_full, preferred_element_type=jnp.float32)]
    pallas_call x0 -> x2, Pallas kernels: none -> 160 us  [the longest x1 159 us: layer(): pl.pallas_call(body, out_shape=(S(x.shape, BF16), S(x.shape, BF16), S((GR...]
    psum x1 -> x0, blocking collectives: 80.5 us -> none  [local(): lax.psum(owned[0].astype(jnp.bfloat16), 'rep').astype(jnp.float32)]
    reshape x21 -> x0, local copies, waits for them, and re-layouts: 69.2 us -> none  [the longest x8 43.6 us: heads_view(): return tensor.reshape(images, length, HEADS, HEAD_DIM)]
    reduce_scatter x2 -> x0, waiting for transfers between devices: 35 us -> none  [sent_together(): lax.psum_scatter(both, axis, scatter_dimension=dim, tiled=True)]
    convert_element_type x19 -> x0, other arithmetic: 29.5 us -> none  [the longest x1 10.9 us: local(): score_grad = (probs_float * (prob_grad - inner)).astype(jnp.bfloat16)]
    reduce_sum x8 -> x0, other arithmetic: 21.1 us -> none  [the longest x1 8.83 us: local(): totals = jnp.sum(expo, axis=-1, keepdims=True)]
  transfers between devices with their start and end apart: 6 -> 0, of which waited for: 3 -> 0; matrix products, arithmetic and copies ran while one was open for 21% -> 0% of each run, Pallas kernels for 0% -> 0%
where the time goes in v1:
time: 171 us; the launch traced here: 170 us
  Pallas kernels  160 us (94%)
  local copies, waits for them, and re-layouts  7.74 us (5%)
    pallas_call x1, Pallas kernels, layer(): pl.pallas_call(body, out_shape=(S(x.shape, BF16), S(x.shape, BF16), S((GR...  159 us
    unnamed x8, local copies, waits for them, and re-layouts  6.13 us

profile of v1, /device:TPU:2, one launch (start us, length us, event | category | flops | bytes accessed | tf_op | source)
XLA Modules:
  0.0 169.8 jit_solution(5967469978627288218)
XLA Ops:
  0.6 0.8 stack.27
  1.4 0.1 tile.21
  1.6 0.7 tile.8
  2.2 0.1 tile.9
  2.3 1.4 select_select_fusion.vin_ref
  3.7 158.6 %shard_map.245 = (bf16[12,197,384]{2,1,0:T(8,128)(2,1)}, bf16[12,197,384]{2,1,0:T(8,128)(2,1)}, bf16[3584,128]{1,0:T(8,128)(2,1)}, bf16[16,128]{1,0:T(8,128)(2,1)}) custom-call(bf16[12,197,384]{2,1,0:T(8,128)(2,1)} %x_ref.1, bf16[12,197,384]{2,1,0:T(8,128)(2,1)} %dy_ref.1, bf16[16,384]{1,0:T(8,128)(2,1)} %select_select_fusion.vin_ref, ...), custom_call_target="tpu_custom_call" | custom-call | tf_op jit(solution)/shard_map/pallas_call | solution.py:489
  162.3 0.0 copy-start
  162.3 1.2 copy-done
  163.5 0.0 copy-start.1
  163.5 0.7 copy-done.1
  164.2 1.4 shard_map.246
  165.5 0.0 copy-start.2
  165.5 3.1 %copy.30 = bf16[12,197,384]{2,1,0:T(8,128)(2,1)} copy(bf16[12,197,384]{2,1,0:T(8,128)(2,1)} %get-tuple-element.62) | data formatting | bytes 3631104
  168.6 0.0 copy-done.2
  168.6 1.2 copy.31
  (5 shorter events, 0.1 us)
Async XLA Ops:
  162.3 1.2 copy-start
  163.5 0.7 copy-start.1
  165.5 3.1 %copy-start.2 = (bf16[12,197,384]{2,1,0:T(8,128)(2,1)S(1)}, bf16[12,197,384]{2,1,0:T(8,128)(2,1)}, u32[]{:S(2)}) copy-start(bf16[12,197,384]{2,1,0:T(8,128)(2,1)} %get-tuple-element.63) | copy-start | bytes 5446660

commit v2 on v1

--- a/solution.py
+++ b/solution.py
@@ -39,28 +39,20 @@
 
 
 def gelu_both(u):
-    a = jnp.abs(u)
-    d = 1.0 + (0.3275911 * math.sqrt(0.5)) * a
-    t = 1.0 / d
+    phi = 0.5 + 0.5 * lax.erf(u * math.sqrt(0.5))
     e = jnp.exp2(u * u * (-0.5 * math.log2(math.e)))
-    p = (0.5 * 1.061405429) * t - (0.5 * 1.453152027)
-    p = p * t + (0.5 * 1.421413741)
-    p = p * t - (0.5 * 0.284496736)
-    p = p * t + (0.5 * 0.254829592)
-    tail = p * t * e
-    phi = jnp.where(u < 0, tail, 1.0 - tail)
     return u * phi, phi + u * (e * (1.0 / math.sqrt(2 * math.pi)))
 
 
 def colsum(v):
     return jnp.sum(v, axis=0, keepdims=True)
 
-CH1, CH2, CH4 = 2, 2, 2
+CH1, CH2, CH4, FC = 2, 2, 2, 512
 MESH = pl.DeviceIdType.MESH
 
-UP_ROW, DOWN_ROW, OUT_ROW, QKV_ROW = 0, 1152, 2304, 2592
+DOWN_ROW, UP_ROW, OUT_ROW, QKV_ROW = 0, 1152, 2304, 2592
 GROWS = 3584
-GROUPS = ((0, 160), (2560, 32), (3072, 32))
+GROUPS = ((0, 64), (1024, 96), (2560, 32), (3072, 32))
 
 
 class Comm:
@@ -81,11 +73,12 @@
             q = pz * 4 + py
             self.planes.append(((q * 2 + self.lo, shard), q))
 
-    def barrier(self):
+    def barrier(self, meanwhile):
         sem = pltpu.get_barrier_semaphore()
         peers = [self.sibling] + [d for d, _ in self.row] + [d for d, _ in self.planes]
         for dev in peers:
             pl.semaphore_signal(sem, inc=1, device_id=dev, device_id_type=MESH)
+        meanwhile()
         pl.semaphore_wait(sem, len(peers))
 
     def copy(self, src, dst, slot, dev):
@@ -178,12 +171,13 @@
     return tmp[...]
 
 
-def body(x_ref, dy_ref, vin_ref, wqkv_in, wo_in, wup_in, wd_in,
+def body(x_ref, dy_ref, g1_in, s1_in, wqkv_in, qv_in, wo_in, bo_in, g2_in, s2_in, wup_in, bup_in,
+         wd_in, bd_in,
          out_ref, ig_ref, fin_ref, finv_ref,
-         stage, out_sem, tmp, dys, dyT, tT, h1s, qkv, ps, cs, h2s, gs, dus, dbs,
+         stage, out_sem, packed, vin_ref, tmp, gub, dys, dyT, tT, h1s, qkv, ps, cs, h2s, gs, dus, dbs,
          vecs_all, wqkv, wo, wup, wd, vec_ref, gvec, grads, gradv,
          rcore0, rplane0, part0, rrow0, rcore1, rplane1, part1, rrow1,
-         rcore2, rplane2, part2, rrow2, rcorev, rplanev, partv, rrowv, fin, finv, ssem, rsem):
+         rcore2, rplane2, part2, rrow2, rcore3, rplane3, part3, rrow3, rcorev, rplanev, partv, rrowv, fin, finv, ssem, rsem):
     dy_copy = pltpu.make_async_copy(dy_ref, stage, out_sem)
     dy_copy.start()
     comm = Comm(ssem, rsem)
@@ -195,17 +189,50 @@
         return full.at[pl.ds(pl.multiple_of(s * n, 16), n)]
 
     params = ((wqkv_in, wqkv), (vin_ref, vecs_all), (wo_in, wo), (wup_in, wup), (wd_in, wd))
-    for own, full in params:
-        n = own.shape[0]
-        full[pl.ds(pl.multiple_of(shard * n, 16), n), :] = own[...]
-    comm.barrier()
+    def meanwhile():
+        packed[...] = jnp.zeros_like(packed)
+        for row, ref in enumerate((g1_in, s1_in, bo_in, g2_in, s2_in, bd_in)):
+            packed[row, 0:96] = ref[...].astype(F32)
+        packed[6, 0:192] = qv_in[...].astype(F32)
+        packed[7, :] = bup_in[...].astype(F32)
+        row = lax.broadcasted_iota(jnp.int32, (16, 1), 0)
+        own = packed[...]
+        six = jnp.where(row < 6, pltpu.roll(own, 96 * shard, 1), 0.0)
+        two = pltpu.roll(own, 192 * comm.core, 1)[6:7, :]
+        two = jnp.where(row == 6 + 2 * comm.hi, two, 0.0)
+        up = jnp.where(row == 9 + shard, own[7:8, :], 0.0)
+        vin_ref[...] = (six + two + up).astype(BF16)
+        for own, full in params:
+            n = own.shape[0]
+            full[pl.ds(pl.multiple_of(shard * n, 16), n), :] = own[...]
+        tmp[...] = jnp.zeros_like(tmp)
+        gvec[...] = jnp.zeros_like(gvec)
+        gub[...] = jnp.zeros_like(gub)
+        for t in (dys, h1s, cs, h2s, gs, dus, dbs, qkv):
+            t[ROWS:TROWS, :] = jnp.zeros((TROWS - ROWS, t.shape[1]), t.dtype)
+        grads[:, :, QKV_ROW + 864:, :] = jnp.zeros((2, 2, GROWS - QKV_ROW - 864, 128), BF16)
+        dy_copy.wait()
+
+        @pl.loop(0, NI)
+        def _(i):
+            r = pl.ds(pl.multiple_of(i * PAD, 16), PAD)
+            dy = padded(stage, i, tmp)
+            dys[r, :] = dy.astype(BF16)
+            gvec[5:6, :] += colsum(dy)
+
+    comm.barrier(meanwhile)
     first, second, third = [], [], []
     for j, (own, full) in enumerate(params):
         first.append(comm.copy(own, place(full, shard), 3 * j, comm.across))
         second.append(comm.copy(own, place(full, shard), 3 * j + 1, comm.sibling))
         third.append(comm.copy(place(full, theirs), place(full, theirs), 3 * j + 2, comm.sibling))
+
+    def send(j):
         first[j].start()
         second[j].start()
+
+    send(1)
+    send(0)
 
     def forward(j):
         first[j].wait_recv()
@@ -218,8 +245,8 @@
     red = [Reduce(comm, 16 + 40 * g, grads, fin, start, n, *bufs)
            for g, ((start, n), bufs) in enumerate(zip(GROUPS, (
                (rcore0, rplane0, part0, rrow0), (rcore1, rplane1, part1, rrow1),
-               (rcore2, rplane2, part2, rrow2))))]
-    redv = Reduce(comm, 136, gradv, finv, 0, 16, rcorev, rplanev, partv, rrowv, scatter=False)
+               (rcore2, rplane2, part2, rrow2), (rcore3, rplane3, part3, rrow3))))]
+    redv = Reduce(comm, 176, gradv, finv, 0, 16, rcorev, rplanev, partv, rrowv, scatter=False)
 
     def vec(r):
         return vec_ref[r:r + 1, :]
@@ -227,21 +254,13 @@
     def vcat(r, n):
         return jnp.concatenate([vec_ref[r + j:r + j + 1, :] for j in range(n)], axis=1)
 
-    tmp[...] = jnp.zeros_like(tmp)
-    gvec[...] = jnp.zeros_like(gvec)
-    for s in (dys, h1s, cs, h2s, gs, dus, dbs, qkv):
-        s[ROWS:TROWS, :] = jnp.zeros((TROWS - ROWS, s.shape[1]), s.dtype)
-    grads[:, :, QKV_ROW + 864:, :] = jnp.zeros((2, 2, GROWS - QKV_ROW - 864, 128), BF16)
-    dy_copy.wait()
-
-    @pl.loop(0, NI)
-    def _(i):
-        r = pl.ds(pl.multiple_of(i * PAD, 16), PAD)
-        dy = padded(stage, i, tmp)
-        dys[r, :] = dy.astype(BF16)
-        gvec[5:6, :] += colsum(dy)
-
-    forward(0)
+    def transpose_into(dst, src):
+        @pl.loop(0, TROWS // 256)
+        def _(b):
+            r = pl.ds(pl.multiple_of(b * 256, 256), 256)
+            dst[:, r] = src[r, :].T
+
+    transpose_into(dyT, dys)
     forward(1)
     gathered(1)
     vec_ref[...] = (
@@ -249,24 +268,23 @@
         + vecs_all[32:48, :].astype(F32) + vecs_all[48:64, :].astype(F32)
     )
 
-    @pl.loop(0, NI)
-    def _(i):
-        r = pl.ds(pl.multiple_of(i * PAD, 16), PAD)
-        n, _ = norm_parts(padded(x_ref, i, tmp))
-        h1s[r, :] = (n * vec(0) + vec(1)).astype(BF16)
-
-    def transpose_into(dst, src):
-        @pl.loop(0, TROWS // 256)
-        def _(b):
-            r = pl.ds(pl.multiple_of(b * 256, 256), 256)
-            dst[:, r] = src[r, :].T
-
-    transpose_into(dyT, dys)
+    def first_norm(a, b):
+        @pl.loop(a, b)
+        def _(i):
+            r = pl.ds(pl.multiple_of(i * PAD, 16), PAD)
+            n, _ = norm_parts(padded(x_ref, i, tmp))
+            h1s[r, :] = (n * vec(0) + vec(1)).astype(BF16)
+
+    first_norm(0, 9)
+    forward(0)
+    for j in (2, 3, 4):
+        send(j)
+    first_norm(9, 12)
     gathered(0)
 
     lane = lax.broadcasted_iota(jnp.int32, (1, 128), 1)
     halves = (lane < 64, lane >= 64)
-    keycol = lax.broadcasted_iota(jnp.int32, (1, PAD), 1) < SEQ
+    lastcol = lax.broadcasted_iota(jnp.int32, (1, PAD - 128), 1) < SEQ - 128
     zero = jnp.zeros((), BF16)
 
     def half(v, h):
@@ -283,25 +301,22 @@
         @pl.loop(first_image, last_image)
         def _(i):
             r = pl.ds(pl.multiple_of(i * PAD, 16), PAD)
+            q, k, v = ([qkv[r, j * D + 128 * p:j * D + 128 * p + 128] for p in range(3)] for j in range(3))
+            ss = [mm_nt(q[h // 2], half(k[h // 2], h % 2)) for h in range(6)]
+            pr = []
+            for h in range(6):
+                s = jnp.concatenate([ss[h][:, 0:128], jnp.where(lastcol, ss[h][:, 128:PAD], -1e30)], axis=1)
+                e = jnp.exp(s - jnp.max(s, axis=-1, keepdims=True))
+                pr.append((e * (1.0 / jnp.sum(e, axis=-1, keepdims=True))).astype(BF16))
+                ps[i * HEADS + h] = pr[h]
             for p in range(3):
-                q = qkv[r, 128 * p:128 * p + 128]
-                k = qkv[r, D + 128 * p:D + 128 * p + 128]
-                v = qkv[r, 2 * D + 128 * p:2 * D + 128 * p + 128]
-                acc = None
-                for h in range(2):
-                    s = mm_nt(q, half(k, h))
-                    s = jnp.where(keycol, s, -1e30)
-                    e = jnp.exp(s - jnp.max(s, axis=-1, keepdims=True))
-                    pr = (e * (1.0 / jnp.sum(e, axis=-1, keepdims=True))).astype(BF16)
-                    ps[i * HEADS + 2 * p + h] = pr
-                    o = mm(pr, half(v, h))
-                    acc = o if acc is None else acc + o
+                acc = mm(pr[2 * p], half(v[p], 0)) + mm(pr[2 * p + 1], half(v[p], 1))
                 cs[r, 128 * p:128 * p + 128] = acc.astype(BF16)
 
-    attention(0, 6)
+    attention(0, 9)
     forward(2)
-    attention(6, 12)
     forward(3)
+    attention(9, 12)
     forward(4)
     for j in (2, 3, 4):
         gathered(j)
@@ -315,17 +330,18 @@
         h2 = (n2 * vec(3) + vec(4)).astype(BF16)
         h2s[r, :] = h2
         dy = dys[r, :]
+        bup = vcat(9, 4)
         acc, dh = x1 + vec(5), None
-        for f in range(4):
-            fc = slice(f * D, f * D + D)
-            u = mm(h2, wup[:, fc]) + vec(9 + f)
+        for f in range(FF // FC):
+            fc = slice(f * FC, f * FC + FC)
+            u = mm(h2, wup[:, fc]) + bup[:, fc]
             g, gp = gelu_both(u)
             g = g.astype(BF16)
             gs[r, fc] = g
             acc = acc + mm(g, wd[fc, :])
             du = (mm_nt(dy, wd[fc, :]) * gp).astype(BF16)
             dus[r, fc] = du
-            gvec[9 + f:10 + f, :] += colsum(du.astype(F32))
+            gub[0:1, fc] += colsum(du.astype(F32))
             o = mm_nt(du, wup[:, fc])
             dh = o if dh is None else dh + o
         for j in range(CH2):
@@ -356,62 +372,64 @@
             for b in range(3):
                 grads[core, h, DOWN_ROW + 384 * b:DOWN_ROW + 384 * b + 384, :] = value[:, 128 * b:128 * b + 128]
 
+    red[0].send_core()
     transpose_into(tT, h2s)
 
-    @pl.loop(0, 4)
+    @pl.loop(0, FF // FC)
     def _(n):
-        cc = pl.ds(pl.multiple_of(n * 384, 128), 384)
-        put(mm(tT[...], dus[:, cc]), UP_ROW + 288 * n)
+        cc = pl.ds(pl.multiple_of(n * FC, 128), FC)
+        put(mm(tT[...], dus[:, cc]), UP_ROW + 3 * FC // 4 * n)
+
+    red[0].send_planes()
 
     transpose_into(tT, cs)
     put(mm(tT[...], dbs[...]), OUT_ROW)
-    red[0].send_core()
+    red[1].send_core()
     transpose_into(tT, h1s)
 
     def attention_back(p):
         sl = [slice(j * D + 128 * p, j * D + 128 * p + 128) for j in range(3)]
 
-        @pl.loop(0, NI)
-        def _(i):
-            r = pl.ds(pl.multiple_of(i * PAD, 16), PAD)
-            q, k, v = (qkv[r, s] for s in sl)
-            dc = dys[r, 128 * p:128 * p + 128]
-            dq = dk = dv = None
-            for h in range(2):
-                pr = ps[i * HEADS + 2 * p + h]
-                da = mm_nt(dc, half(v, h))
-                prf = pr.astype(F32)
-                t = prf * da
-                ds = (t - prf * jnp.sum(t, axis=-1, keepdims=True)).astype(BF16)
-                ov = mm_tn(pr, half(dc, h))
-                oq = mm(ds, half(k, h))
-                ok = mm_tn(ds, half(q, h))
-                if dq is None:
-                    dq, dk, dv = oq, ok, ov
-                else:
-                    dq, dk, dv = dq + oq, dk + ok, dv + ov
-            for j, o in enumerate((dq * 0.125, dk, dv)):
-                o = o.astype(BF16)
-                qkv[r, sl[j]] = o
-                if j != 1:
-                    gvec[6 + j:7 + j, 128 * p:128 * p + 128] += colsum(o.astype(F32))
+        @pl.loop(0, NI // 3)
+        def _(c):
+            rs = [pl.ds(pl.multiple_of((3 * c + m) * PAD, 16), PAD) for m in range(3)]
+            q, k, v = ([qkv[r, t] for r in rs] for t in sl)
+            dc = [dys[r, 128 * p:128 * p + 128] for r in rs]
+            pr = [ps.at[(3 * c + m) * HEADS + 2 * p + h] for m in range(3) for h in range(2)]
+            das = [mm_nt(dc[m // 2], half(v[m // 2], m % 2)) for m in range(6)]
+            dss = []
+            for m in range(6):
+                prf = pr[m][...].astype(F32)
+                t = prf * das[m]
+                dss.append((t - prf * jnp.sum(t, axis=-1, keepdims=True)).astype(BF16))
+            for m in range(3):
+                a, b = 2 * m, 2 * m + 1
+                dv = mm_tn(pr[a][...], half(dc[m], 0)) + mm_tn(pr[b][...], half(dc[m], 1))
+                dq = mm(dss[a], half(k[m], 0)) + mm(dss[b], half(k[m], 1))
+                dk = mm_tn(dss[a], half(q[m], 0)) + mm_tn(dss[b], half(q[m], 1))
+                for j, o in enumerate((dq * 0.125, dk, dv)):
+                    o = o.astype(BF16)
+                    qkv[rs[m], sl[j]] = o
+                    if j != 1:
+                        gvec[6 + j:7 + j, 128 * p:128 * p + 128] += colsum(o.astype(F32))
 
     def qkv_grad(p):
         rhs = jnp.concatenate([qkv[:, j * D + 128 * p:j * D + 128 * p + 128] for j in range(3)], axis=1)
         put(mm(tT[...], rhs), QKV_ROW + 288 * p)
 
     attention_back(0)
-    red[0].send_planes()
+    red[1].send_planes()
     qkv_grad(0)
     attention_back(1)
     red[0].send_row()
     qkv_grad(1)
-    red[1].send_core()
+    red[2].send_core()
     attention_back(2)
     red[0].send_back()
-    red[1].send_planes()
+    red[2].send_planes()
     qkv_grad(2)
-    red[2].send_core()
+    red[3].send_core()
+    red[1].send_row()
     out_copy.wait()
 
     def first_norm_back(a, b):
@@ -428,13 +446,16 @@
                 stage[c * CH4 + j] = ig[j * PAD:j * PAD + SEQ].astype(BF16)
 
     first_norm_back(0, 4)
-    red[2].send_planes()
+    red[3].send_planes()
     first_norm_back(4, 8)
-    red[1].send_row()
+    red[1].send_back()
+    red[2].send_row()
     first_norm_back(8, 12)
 
     ig_copy = pltpu.make_async_copy(stage, ig_ref, out_sem)
     ig_copy.start()
+    for b in range(4):
+        gvec[9 + b:10 + b, :] = gub[0:1, b * D:b * D + D]
     gv = gvec[...]
     for s in range(4):
         moved = gv if s == 0 else pltpu.roll(gv, D - 96 * s, 1)
@@ -447,12 +468,12 @@
         )
         gradv[s % 2, s // 2] = tile.astype(BF16)
     redv.send_core()
-    red[2].send_row()
+    red[3].send_row()
     redv.send_planes()
-    red[1].send_back()
     red[2].send_back()
+    red[3].send_back()
     redv.send_row()
-    for g in (0, 1, 2):
+    for g in range(4):
         red[g].finish()
     redv.send_back()
     fin_ref[...] = fin[...]
@@ -467,11 +488,11 @@
 def scratches():
     V = pltpu.VMEM
     bufs = []
-    for n, full in ((160, 2560), (32, 512), (32, 512), (16, 16)):
+    for n, full in ((64, 1024), (96, 1536), (32, 512), (32, 512), (16, 16)):
         bufs += [V((2, full, 128), BF16), V((15, 2, n, 128), BF16), V((2, n, 128), BF16), V((3, n, 128), BF16)]
     return [
         V((NI, SEQ, D), BF16), pltpu.SemaphoreType.DMA,
-        V((PAD, D), F32), V((TROWS, D), BF16), V((D, TROWS), BF16), V((D, TROWS), BF16),
+        V((16, D), F32), V((16, D), BF16), V((PAD, D), F32), V((8, FF), F32), V((TROWS, D), BF16), V((D, TROWS), BF16), V((D, TROWS), BF16),
         V((TROWS, D), BF16), V((TROWS, 3 * D), BF16), V((NI * HEADS, PAD, PAD), BF16),
         V((TROWS, D), BF16), V((TROWS, D), BF16), V((TROWS, FF), BF16), V((TROWS, FF), BF16),
         V((TROWS, D), BF16),
@@ -479,24 +500,27 @@
         V((16, D), F32), V((16, D), F32), V((2, 2, GROWS, 128), BF16), V((2, 2, 16, 128), BF16),
         *bufs,
         V((GROWS, 128), BF16), V((16, 128), BF16),
-        pltpu.SemaphoreType.DMA((160,)), pltpu.SemaphoreType.DMA((160,)),
+        pltpu.SemaphoreType.DMA((200,)), pltpu.SemaphoreType.DMA((200,)),
     ]
 
 
-def layer(x, dy, vecs, wqkv, wo, wup, wd):
+def layer(x, dy, *params):
     S = jax.ShapeDtypeStruct
     vm, hbm = pl.BlockSpec(memory_space=pltpu.VMEM), pl.BlockSpec(memory_space=pl.ANY)
     return pl.pallas_call(
         body,
         out_shape=(S(x.shape, BF16), S(x.shape, BF16), S((GROWS, 128), BF16), S((16, 128), BF16)),
-        in_specs=[vm, hbm] + [vm] * 5, out_specs=(hbm, hbm, vm, vm),
+        in_specs=[vm, hbm] + [vm] * 12, out_specs=(hbm, hbm, vm, vm),
         scratch_shapes=scratches(),
         compiler_params=pltpu.CompilerParams(
             vmem_limit_bytes=int(63.5 * 2**20), collective_id=0, has_side_effects=True),
-    )(x, dy, vecs, wqkv, wo, wup, wd)
-
-
-def unpack_body(fin, finv, g1, s1, gqkv, gqv, go, bo, g2, s2, gup, bup, gd, bd):
+    )(x, dy, *params)
+
+
+def unpack_body(out_in, ig_in, fin, finv, out, ig, g1, s1, gqkv, gqv, go, bo, g2, s2, gup, bup, gd, bd, sems):
+    copies = [pltpu.make_async_copy(out_in, out, sems.at[0]), pltpu.make_async_copy(ig_in, ig, sems.at[1])]
+    for copy in copies:
+        copy.start()
     for b in range(12):
         gup[:, 128 * b:128 * b + 128] = fin[UP_ROW + 96 * b:UP_ROW + 96 * b + 96, :].astype(F32)
     for b in range(3):
@@ -513,36 +537,28 @@
     gqv[128:192] = v[7, 0:64]
     for b in range(3):
         bup[128 * b:128 * b + 128] = v[8 + b, :]
-
-
-def unpack(fin, finv):
+    for copy in copies:
+        copy.wait()
+
+
+def unpack(outputs, input_grad, fin, finv):
     def S(*shape):
         return jax.ShapeDtypeStruct(shape, F32)
 
-    vm = pl.BlockSpec(memory_space=pltpu.VMEM)
+    vm, hbm = pl.BlockSpec(memory_space=pltpu.VMEM), pl.BlockSpec(memory_space=pl.ANY)
+    whole = jax.ShapeDtypeStruct(outputs.shape, BF16)
     return pl.pallas_call(
         unpack_body,
-        out_shape=(S(96), S(96), S(96, 3 * D), S(192), S(96, D), S(96), S(96), S(96),
+        out_shape=(whole, whole, S(96), S(96), S(96, 3 * D), S(192), S(96, D), S(96), S(96), S(96),
                    S(96, FF), S(384), S(384, D), S(96)),
-        in_specs=[vm] * 2, out_specs=(vm,) * 12,
+        in_specs=[hbm, hbm, vm, vm], out_specs=(hbm, hbm) + (vm,) * 12,
+        scratch_shapes=[pltpu.SemaphoreType.DMA((2,))],
         compiler_params=pltpu.CompilerParams(vmem_limit_bytes=24 * 2**20),
-    )(fin, finv)
-
-
-def local(inputs, out_grad, ln1_gain, ln1_shift, qkv_weight, qv_bias, out_weight, out_bias,
-          ln2_gain, ln2_shift, up_weight, up_bias, down_weight, down_bias):
-    shard = lax.axis_index("shard")
-    lane = jnp.arange(D)
-    six = jnp.stack([ln1_gain, ln1_shift, out_bias, ln2_gain, ln2_shift, down_bias])
-    six = jnp.where(lane // 96 == shard, jnp.tile(six, (1, 4)), 0)
-    two = jnp.where(lane // 192 == shard % 2, jnp.tile(qv_bias, 2), 0)
-    row = jnp.arange(16)[:, None]
-    vecs = jnp.concatenate([six, jnp.zeros((10, D), BF16)])
-    vecs = jnp.where(row == 6 + 2 * (shard // 2), two, vecs)
-    vecs = jnp.where(row == 9 + shard, up_bias, vecs)
-    outputs, input_grad, fin, finv = layer(
-        inputs, out_grad, vecs, qkv_weight, out_weight, up_weight, down_weight)
-    return (outputs, input_grad, *unpack(fin, finv))
+    )(outputs, input_grad, fin, finv)
+
+
+def local(*arrays):
+    return unpack(*layer(*arrays))
 
 
 def solution(mesh):

time: 171 us -> 125 us (0.73)
  Pallas kernels: 160 us -> 118 us
  local copies, waits for them, and re-layouts: 7.74 us -> 4.86 us
    pallas_call x1, Pallas kernels: 159 us -> 115 us  [layer(): pl.pallas_call(body, out_shape=(S(x.shape, BF16), S(x.shape, BF16), S((GR...]
    pallas_call x1, Pallas kernels: 1.35 us -> 3.1 us  [unpack(): pl.pallas_call(unpack_body, out_shape=(whole, whole, S(96), S(96), S(96,...]
where the time goes in v2:
time: 125 us; the launch traced here: 124 us
  Pallas kernels  118 us (94%)
  local copies, waits for them, and re-layouts  4.86 us (4%)
    pallas_call x1, Pallas kernels, layer(): pl.pallas_call(body, out_shape=(S(x.shape, BF16), S(x.shape, BF16), S((GR...  115 us
    unnamed x8, local copies, waits for them, and re-layouts  4.86 us
    pallas_call x1, Pallas kernels, unpack(): pl.pallas_call(unpack_body, out_shape=(whole, whole, S(96), S(96), S(96,...  3.1 us

profile of v2, /device:TPU:2, one launch (start us, length us, event | category | flops | bytes accessed | tf_op | source)
XLA Modules:
  0.0 123.8 jit_solution(5619511071088421496)
XLA Ops:
  0.7 115.1 %shard_map.245 = (bf16[12,197,384]{2,1,0:T(8,128)(2,1)}, bf16[12,197,384]{2,1,0:T(8,128)(2,1)}, bf16[3584,128]{1,0:T(8,128)(2,1)}, bf16[16,128]{1,0:T(8,128)(2,1)}) custom-call(bf16[12,197,384]{2,1,0:T(8,128)(2,1)} %x_ref.1, bf16[12,197,384]{2,1,0:T(8,128)(2,1)} %dy_ref.1, bf16[96]{0:T(256)(128)(2,1)} %g1_in.1, bf16[96]{0:T(256)(128)(2,1)} %s1_in.1, ...), custom_call_target="tpu_custom_call" | custom-call | tf_op jit(solution)/shard_map/pallas_call | solution.py:510
  115.7 0.0 copy-start
  115.7 1.5 %copy-done = bf16[12,197,384]{2,1,0:T(8,128)(2,1)S(1)} copy-done((bf16[12,197,384]{2,1,0:T(8,128)(2,1)S(1)}, bf16[12,197,384]{2,1,0:T(8,128)(2,1)}, u32[]{:S(2)}) %copy-start) | copy-done | bytes 1815576
  117.2 0.0 copy-start.1
  117.2 1.5 %copy-done.1 = bf16[12,197,384]{2,1,0:T(8,128)(2,1)S(1)} copy-done((bf16[12,197,384]{2,1,0:T(8,128)(2,1)S(1)}, bf16[12,197,384]{2,1,0:T(8,128)(2,1)}, u32[]{:S(2)}) %copy-start.1) | copy-done | bytes 1815576
  118.7 0.0 copy-start.2
  118.7 1.2 copy-done.2
  119.9 0.0 copy-start.3
  119.9 0.7 copy-done.3
  120.6 3.1 %shard_map.246 = (bf16[12,197,384]{2,1,0:T(8,128)(2,1)}, bf16[12,197,384]{2,1,0:T(8,128)(2,1)}, f32[96]{0:T(128)}, f32[96]{0:T(128)}, f32[96,1152]{1,0:T(8,128)}...) custom-call(bf16[12,197,384]{2,1,0:T(8,128)(2,1)S(1)} %copy-done, ...), custom_call_target="tpu_custom_call" | custom-call | tf_op jit(solution)/shard_map/pallas_call | solution.py:550
Async XLA Ops:
  115.7 1.5 %copy-start = (bf16[12,197,384]{2,1,0:T(8,128)(2,1)S(1)}, bf16[12,197,384]{2,1,0:T(8,128)(2,1)}, u32[]{:S(2)}) copy-start(bf16[12,197,384]{2,1,0:T(8,128)(2,1)} %get-tuple-element.18.out_in) | copy-start | bytes 5446660
  117.2 1.5 %copy-start.1 = (bf16[12,197,384]{2,1,0:T(8,128)(2,1)S(1)}, bf16[12,197,384]{2,1,0:T(8,128)(2,1)}, u32[]{:S(2)}) copy-start(bf16[12,197,384]{2,1,0:T(8,128)(2,1)} %get-tuple-element.19.ig_in) | copy-start | bytes 5446660
  118.7 1.2 copy-start.2
  119.9 0.7 copy-start.3

commit v3 on v2

--- a/solution.py
+++ b/solution.py
@@ -52,7 +52,8 @@
 
 DOWN_ROW, UP_ROW, OUT_ROW, QKV_ROW = 0, 1152, 2304, 2592
 GROWS = 3584
-GROUPS = ((0, 64), (1024, 96), (2560, 32), (3072, 32))
+SPREAD = ((0, 32), (1024, 48), (2560, 16))
+LAST = (3072, 32)
 
 
 class Comm:
@@ -63,10 +64,13 @@
         self.hi, self.core, self.plane = shard // 2, shard % 2, rep // 2
         self.sibling = (rep, self.hi * 2 + 1 - self.core)
         self.across = (self.plane * 2 + 1 - self.lo, (1 - self.hi) * 2 + self.core)
-        self.row = []
+        self.mate = (self.plane * 2 + 1 - self.lo, shard)
+        self.row, self.quarters = [], []
         for dh, dl in ((0, 1), (1, 0), (1, 1)):
             ph, plo = (self.hi + dh) % 2, (self.lo + dl) % 2
-            self.row.append(((self.plane * 2 + plo, ph * 2 + self.core), ph))
+            dev = (self.plane * 2 + plo, ph * 2 + self.core)
+            self.row.append((dev, ph))
+            self.quarters.append((dev, ph, plo))
         self.planes = []
         for d in range(1, 16):
             pz, py = (self.z + d // 4) % 4, (self.y + d % 4) % 4
@@ -166,6 +170,86 @@
             cp.wait()
 
 
+class Spread:
+    def __init__(self, comm, base, grads, fin, start, m, rcore, rrow, rplane):
+        c = self.c = comm
+        self.grads, self.fin, self.rcore, self.rrow, self.rplane = grads, fin, rcore, rrow, rplane
+        self.start, self.half = start, 16 * m
+        self.core_copy = c.copy(grads.at[1 - c.core, :, pl.ds(start, 32 * m), :], rcore, base, c.sibling)
+
+        def rows(lo):
+            return pl.ds(pl.multiple_of(start + lo * self.half, 16), self.half)
+
+        def piece(q):
+            return pl.ds(pl.multiple_of(start + c.lo * self.half + q * m, 16), m)
+
+        self.rows, self.mine = rows, piece(c.plane)
+        self.row_copies = [
+            c.copy(grads.at[c.core, h, rows(lo), :], rrow.at[d], base + 1 + d, dev)
+            for d, (dev, h, lo) in enumerate(c.quarters)
+        ]
+        self.plane_copies = [
+            c.copy(grads.at[c.core, c.hi, piece(q), :], rplane.at[d], base + 4 + d, dev)
+            for d, (dev, q) in enumerate(c.planes)
+        ]
+        self.back_copies = [
+            c.copy(fin.at[self.mine, :], fin.at[self.mine, :], base + 19 + d, dev)
+            for d, (dev, q) in enumerate(c.planes)
+        ]
+        self.mate_copy = c.copy(fin.at[rows(c.lo), :], fin.at[rows(c.lo), :], base + 34, c.mate)
+
+    def send_core(self):
+        self.core_copy.start()
+
+    def send_row(self):
+        self.core_copy.wait()
+
+        @pl.loop(0, 2 * self.half // 256)
+        def _(b):
+            off = pl.multiple_of(b * 256, 256)
+            r = pl.ds(pl.multiple_of(self.start + off, 16), 256)
+            for h in range(2):
+                t = self.grads[self.c.core, h, r, :].astype(F32) + self.rcore[h, pl.ds(off, 256), :].astype(F32)
+                self.grads[self.c.core, h, r, :] = t.astype(BF16)
+
+        for cp in self.row_copies:
+            cp.start()
+
+    def send_planes(self):
+        for cp in self.row_copies:
+            cp.wait()
+
+        @pl.loop(0, self.half // 256)
+        def _(b):
+            off = pl.multiple_of(b * 256, 256)
+            r = pl.ds(pl.multiple_of(self.start + self.c.lo * self.half + off, 16), 256)
+            t = self.grads[self.c.core, self.c.hi, r, :].astype(F32)
+            for d in range(3):
+                t = t + self.rrow[d, pl.ds(off, 256), :].astype(F32)
+            self.grads[self.c.core, self.c.hi, r, :] = t.astype(BF16)
+
+        for cp in self.plane_copies:
+            cp.start()
+
+    def send_back(self):
+        for cp in self.plane_copies:
+            cp.wait()
+        t = self.grads[self.c.core, self.c.hi, self.mine, :].astype(F32)
+        for d in range(15):
+            t = t + self.rplane[d].astype(F32)
+        self.fin[self.mine, :] = t.astype(BF16)
+        for cp in self.back_copies:
+            cp.start()
+
+    def send_mate(self):
+        for cp in self.back_copies:
+            cp.wait()
+        self.mate_copy.start()
+
+    def finish(self):
+        self.mate_copy.wait()
+
+
 def padded(ref, i, tmp):
     tmp[0:SEQ, :] = ref[i].astype(F32)
     return tmp[...]
@@ -174,10 +258,10 @@
 def body(x_ref, dy_ref, g1_in, s1_in, wqkv_in, qv_in, wo_in, bo_in, g2_in, s2_in, wup_in, bup_in,
          wd_in, bd_in,
          out_ref, ig_ref, fin_ref, finv_ref,
-         stage, out_sem, packed, vin_ref, tmp, gub, dys, dyT, tT, h1s, qkv, ps, cs, h2s, gs, dus, dbs,
+         stage, out_sem, out_sem2, packed, vin_ref, tmp, gub, dys, dyT, tT, h1s, qkv, ps, cs, h2s, gs, dus, dbs,
          vecs_all, wqkv, wo, wup, wd, vec_ref, gvec, grads, gradv,
-         rcore0, rplane0, part0, rrow0, rcore1, rplane1, part1, rrow1,
-         rcore2, rplane2, part2, rrow2, rcore3, rplane3, part3, rrow3, rcorev, rplanev, partv, rrowv, fin, finv, ssem, rsem):
+         rcore0, rrow0, rplane0, rcore1, rrow1, rplane1, rcore2, rrow2, rplane2,
+         rcore3, rplane3, part3, rrow3, rcorev, rplanev, partv, rrowv, fin, finv, ssem, rsem):
     dy_copy = pltpu.make_async_copy(dy_ref, stage, out_sem)
     dy_copy.start()
     comm = Comm(ssem, rsem)
@@ -221,11 +305,25 @@
             gvec[5:6, :] += colsum(dy)
 
     comm.barrier(meanwhile)
-    first, second, third = [], [], []
+    first, second, third, mate, fourth = [], [], [], [], []
     for j, (own, full) in enumerate(params):
-        first.append(comm.copy(own, place(full, shard), 3 * j, comm.across))
-        second.append(comm.copy(own, place(full, shard), 3 * j + 1, comm.sibling))
-        third.append(comm.copy(place(full, theirs), place(full, theirs), 3 * j + 2, comm.sibling))
+        n = own.shape[0]
+        m = n // 2 if j != 1 else n
+
+        def part(ref, s, which):
+            return ref.at[pl.ds(pl.multiple_of(s * n + which * m, 16), m)]
+
+        out_half, in_half = (1 - comm.lo, comm.lo) if j != 1 else (0, 0)
+        first.append(comm.copy(part(own, 0, out_half), part(full, shard, out_half), 5 * j, comm.across))
+        second.append(comm.copy(own, place(full, shard), 5 * j + 1, comm.sibling))
+        mine, other = part(full, theirs, in_half), part(full, theirs, 1 - in_half)
+        third.append(comm.copy(mine, mine, 5 * j + 2, comm.sibling))
+        if j != 1:
+            mate.append(comm.copy(mine, mine, 5 * j + 3, comm.mate))
+            fourth.append(comm.copy(other, other, 5 * j + 4, comm.sibling))
+        else:
+            mate.append(None)
+            fourth.append(None)
 
     def send(j):
         first[j].start()
@@ -237,16 +335,26 @@
     def forward(j):
         first[j].wait_recv()
         third[j].start()
+        if j != 1:
+            mate[j].start()
+
+    def forward_mate(j):
+        mate[j].wait_recv()
+        fourth[j].start()
 
     def gathered(j):
         second[j].wait_recv()
         third[j].wait_recv()
-
-    red = [Reduce(comm, 16 + 40 * g, grads, fin, start, n, *bufs)
-           for g, ((start, n), bufs) in enumerate(zip(GROUPS, (
-               (rcore0, rplane0, part0, rrow0), (rcore1, rplane1, part1, rrow1),
-               (rcore2, rplane2, part2, rrow2), (rcore3, rplane3, part3, rrow3))))]
-    redv = Reduce(comm, 176, gradv, finv, 0, 16, rcorev, rplanev, partv, rrowv, scatter=False)
+        if j != 1:
+            fourth[j].wait_recv()
+
+    red = [
+        Spread(comm, 25 + 35 * g, grads, fin, start, m, *bufs)
+        for g, ((start, m), bufs) in enumerate(zip(SPREAD, (
+            (rcore0, rrow0, rplane0), (rcore1, rrow1, rplane1), (rcore2, rrow2, rplane2))))
+    ]
+    red.append(Reduce(comm, 130, grads, fin, *LAST, rcore3, rplane3, part3, rrow3))
+    redv = Reduce(comm, 166, gradv, finv, 0, 16, rcorev, rplanev, partv, rrowv, scatter=False)
 
     def vec(r):
         return vec_ref[r:r + 1, :]
@@ -275,11 +383,12 @@
             n, _ = norm_parts(padded(x_ref, i, tmp))
             h1s[r, :] = (n * vec(0) + vec(1)).astype(BF16)
 
-    first_norm(0, 9)
+    first_norm(0, 6)
     forward(0)
     for j in (2, 3, 4):
         send(j)
-    first_norm(9, 12)
+    first_norm(6, 12)
+    forward_mate(0)
     gathered(0)
 
     lane = lax.broadcasted_iota(jnp.int32, (1, 128), 1)
@@ -313,11 +422,17 @@
                 acc = mm(pr[2 * p], half(v[p], 0)) + mm(pr[2 * p + 1], half(v[p], 1))
                 cs[r, 128 * p:128 * p + 128] = acc.astype(BF16)
 
-    attention(0, 9)
+    attention(0, 2)
     forward(2)
     forward(3)
-    attention(9, 12)
+    attention(2, 4)
     forward(4)
+    attention(4, 7)
+    forward_mate(2)
+    forward_mate(3)
+    attention(7, 10)
+    forward_mate(4)
+    attention(10, 12)
     for j in (2, 3, 4):
         gathered(j)
 
@@ -380,8 +495,7 @@
         cc = pl.ds(pl.multiple_of(n * FC, 128), FC)
         put(mm(tT[...], dus[:, cc]), UP_ROW + 3 * FC // 4 * n)
 
-    red[0].send_planes()
-
+    red[0].send_row()
     transpose_into(tT, cs)
     put(mm(tT[...], dbs[...]), OUT_ROW)
     red[1].send_core()
@@ -418,18 +532,19 @@
         put(mm(tT[...], rhs), QKV_ROW + 288 * p)
 
     attention_back(0)
-    red[1].send_planes()
+    red[0].send_planes()
+    red[1].send_row()
     qkv_grad(0)
     attention_back(1)
-    red[0].send_row()
+    red[0].send_back()
     qkv_grad(1)
     red[2].send_core()
     attention_back(2)
-    red[0].send_back()
-    red[2].send_planes()
+    red[1].send_planes()
+    red[0].send_mate()
+    red[2].send_row()
     qkv_grad(2)
     red[3].send_core()
-    red[1].send_row()
     out_copy.wait()
 
     def first_norm_back(a, b):
@@ -445,12 +560,16 @@
             for j in range(CH4):
                 stage[c * CH4 + j] = ig[j * PAD:j * PAD + SEQ].astype(BF16)
 
-    first_norm_back(0, 4)
+    first_norm_back(0, 2)
     red[3].send_planes()
-    first_norm_back(4, 8)
     red[1].send_back()
-    red[2].send_row()
-    first_norm_back(8, 12)
+    first_norm_back(2, 6)
+    red[2].send_planes()
+    red[1].send_mate()
+    first_norm_back(6, 10)
+    red[3].send_row()
+    red[2].send_back()
+    first_norm_back(10, 12)
 
     ig_copy = pltpu.make_async_copy(stage, ig_ref, out_sem)
     ig_copy.start()
@@ -468,30 +587,36 @@
         )
         gradv[s % 2, s // 2] = tile.astype(BF16)
     redv.send_core()
-    red[3].send_row()
+    red[3].send_back()
+    red[2].send_mate()
     redv.send_planes()
-    red[2].send_back()
-    red[3].send_back()
     redv.send_row()
-    for g in range(4):
-        red[g].finish()
+    for group in red:
+        group.finish()
     redv.send_back()
-    fin_ref[...] = fin[...]
+    fin_copy = pltpu.make_async_copy(fin, fin_ref, out_sem2)
+    fin_copy.start()
     finv_ref[...] = finv[...]
     for j in range(5):
         first[j].wait_send()
         second[j].wait_send()
         third[j].wait_send()
+        if j != 1:
+            mate[j].wait_send()
+            fourth[j].wait_send()
     ig_copy.wait()
+    fin_copy.wait()
 
 
 def scratches():
     V = pltpu.VMEM
     bufs = []
-    for n, full in ((64, 1024), (96, 1536), (32, 512), (32, 512), (16, 16)):
+    for _, m in SPREAD:
+        bufs += [V((2, 32 * m, 128), BF16), V((3, 16 * m, 128), BF16), V((15, m, 128), BF16)]
+    for n, full in ((32, 512), (16, 16)):
         bufs += [V((2, full, 128), BF16), V((15, 2, n, 128), BF16), V((2, n, 128), BF16), V((3, n, 128), BF16)]
     return [
-        V((NI, SEQ, D), BF16), pltpu.SemaphoreType.DMA,
+        V((NI, SEQ, D), BF16), pltpu.SemaphoreType.DMA, pltpu.SemaphoreType.DMA,
         V((16, D), F32), V((16, D), BF16), V((PAD, D), F32), V((8, FF), F32), V((TROWS, D), BF16), V((D, TROWS), BF16), V((D, TROWS), BF16),
         V((TROWS, D), BF16), V((TROWS, 3 * D), BF16), V((NI * HEADS, PAD, PAD), BF16),
         V((TROWS, D), BF16), V((TROWS, D), BF16), V((TROWS, FF), BF16), V((TROWS, FF), BF16),
@@ -510,7 +635,7 @@
     return pl.pallas_call(
         body,
         out_shape=(S(x.shape, BF16), S(x.shape, BF16), S((GROWS, 128), BF16), S((16, 128), BF16)),
-        in_specs=[vm, hbm] + [vm] * 12, out_specs=(hbm, hbm, vm, vm),
+        in_specs=[vm, hbm] + [vm] * 12, out_specs=(hbm, hbm, hbm, vm),
         scratch_shapes=scratches(),
         compiler_params=pltpu.CompilerParams(
             vmem_limit_bytes=int(63.5 * 2**20), collective_id=0, has_side_effects=True),
@@ -553,7 +678,7 @@
                    S(96, FF), S(384), S(384, D), S(96)),
         in_specs=[hbm, hbm, vm, vm], out_specs=(hbm, hbm) + (vm,) * 12,
         scratch_shapes=[pltpu.SemaphoreType.DMA((2,))],
-        compiler_params=pltpu.CompilerParams(vmem_limit_bytes=24 * 2**20),
+        compiler_params=pltpu.CompilerParams(vmem_limit_bytes=62 * 2**20),
     )(outputs, input_grad, fin, finv)
 
 

time: 125 us -> 242 us (1.94)
  Pallas kernels: 118 us -> 239 us
  local copies, waits for them, and re-layouts: 4.86 us -> 0 us
    pallas_call x1, Pallas kernels: 3.1 us -> 115 us  [unpack(): pl.pallas_call(unpack_body, out_shape=(whole, whole, S(96), S(96), S(96,...]
    pallas_call x1, Pallas kernels: 115 us -> 124 us  [layer(): pl.pallas_call(body, out_shape=(S(x.shape, BF16), S(x.shape, BF16), S((GR...]
    unnamed x8 -> x0, local copies, waits for them, and re-layouts: 4.86 us -> none
where the time goes in v3:
time: 242 us; the launch traced here: 240 us
  Pallas kernels  239 us (99%)
    pallas_call x1, Pallas kernels, layer(): pl.pallas_call(body, out_shape=(S(x.shape, BF16), S(x.shape, BF16), S((GR...  124 us
    pallas_call x1, Pallas kernels, unpack(): pl.pallas_call(unpack_body, out_shape=(whole, whole, S(96), S(96), S(96,...  115 us

profile of v3, /device:TPU:2, one launch (start us, length us, event | category | flops | bytes accessed | tf_op | source)
XLA Modules:
  0.0 240.3 jit_solution(986096808564938140)
XLA Ops:
  0.7 124.3 %shard_map.245 = (bf16[12,197,384]{2,1,0:T(8,128)(2,1)}, bf16[12,197,384]{2,1,0:T(8,128)(2,1)}, bf16[3584,128]{1,0:T(8,128)(2,1)}, bf16[16,128]{1,0:T(8,128)(2,1)}) custom-call(bf16[12,197,384]{2,1,0:T(8,128)(2,1)} %x_ref.1, bf16[12,197,384]{2,1,0:T(8,128)(2,1)} %dy_ref.1, bf16[96]{0:T(256)(128)(2,1)} %g1_in.1, bf16[96]{0:T(256)(128)(2,1)} %s1_in.1, ...), custom_call_target="tpu_custom_call" | custom-call | tf_op jit(solution)/shard_map/pallas_call | solution.py:635
  124.9 115.2 %shard_map.246 = (bf16[12,197,384]{2,1,0:T(8,128)(2,1)}, bf16[12,197,384]{2,1,0:T(8,128)(2,1)}, f32[96]{0:T(128)}, f32[96]{0:T(128)}, f32[96,1152]{1,0:T(8,128)}...) custom-call(bf16[12,197,384]{2,1,0:T(8,128)(2,1)} %get-tuple-element, ...), custom_call_target="tpu_custom_call" | custom-call | tf_op jit(solution)/shard_map/pallas_call | solution.py:675

commit v4 on v2

--- a/solution.py
+++ b/solution.py
@@ -171,15 +171,17 @@
     return tmp[...]
 
 
-def body(x_ref, dy_ref, g1_in, s1_in, wqkv_in, qv_in, wo_in, bo_in, g2_in, s2_in, wup_in, bup_in,
+def body(x_in, dy_ref, g1_in, s1_in, wqkv_in, qv_in, wo_in, bo_in, g2_in, s2_in, wup_in, bup_in,
          wd_in, bd_in,
          out_ref, ig_ref, fin_ref, finv_ref,
-         stage, out_sem, packed, vin_ref, tmp, gub, dys, dyT, tT, h1s, qkv, ps, cs, h2s, gs, dus, dbs,
+         x_ref, x_sem, stage, out_sem, packed, vin_ref, tmp, gub, dys, dyT, tT, h1s, qkv, ps, cs, h2s, gs, dus, dbs,
          vecs_all, wqkv, wo, wup, wd, vec_ref, gvec, grads, gradv,
          rcore0, rplane0, part0, rrow0, rcore1, rplane1, part1, rrow1,
          rcore2, rplane2, part2, rrow2, rcore3, rplane3, part3, rrow3, rcorev, rplanev, partv, rrowv, fin, finv, ssem, rsem):
     dy_copy = pltpu.make_async_copy(dy_ref, stage, out_sem)
     dy_copy.start()
+    x_copy = pltpu.make_async_copy(x_in, x_ref, x_sem)
+    x_copy.start()
     comm = Comm(ssem, rsem)
     shard = comm.hi * 2 + comm.core
     theirs = (1 - comm.hi) * 2 + comm.core
@@ -275,6 +277,7 @@
             n, _ = norm_parts(padded(x_ref, i, tmp))
             h1s[r, :] = (n * vec(0) + vec(1)).astype(BF16)
 
+    x_copy.wait()
     first_norm(0, 9)
     forward(0)
     for j in (2, 3, 4):
@@ -476,13 +479,15 @@
     for g in range(4):
         red[g].finish()
     redv.send_back()
-    fin_ref[...] = fin[...]
+    fin_copy = pltpu.make_async_copy(fin, fin_ref, x_sem)
+    fin_copy.start()
     finv_ref[...] = finv[...]
     for j in range(5):
         first[j].wait_send()
         second[j].wait_send()
         third[j].wait_send()
     ig_copy.wait()
+    fin_copy.wait()
 
 
 def scratches():
@@ -491,7 +496,7 @@
     for n, full in ((64, 1024), (96, 1536), (32, 512), (32, 512), (16, 16)):
         bufs += [V((2, full, 128), BF16), V((15, 2, n, 128), BF16), V((2, n, 128), BF16), V((3, n, 128), BF16)]
     return [
-        V((NI, SEQ, D), BF16), pltpu.SemaphoreType.DMA,
+        V((NI, SEQ, D), BF16), pltpu.SemaphoreType.DMA, V((NI, SEQ, D), BF16), pltpu.SemaphoreType.DMA,
         V((16, D), F32), V((16, D), BF16), V((PAD, D), F32), V((8, FF), F32), V((TROWS, D), BF16), V((D, TROWS), BF16), V((D, TROWS), BF16),
         V((TROWS, D), BF16), V((TROWS, 3 * D), BF16), V((NI * HEADS, PAD, PAD), BF16),
         V((TROWS, D), BF16), V((TROWS, D), BF16), V((TROWS, FF), BF16), V((TROWS, FF), BF16),
@@ -510,16 +515,25 @@
     return pl.pallas_call(
         body,
         out_shape=(S(x.shape, BF16), S(x.shape, BF16), S((GROWS, 128), BF16), S((16, 128), BF16)),
-        in_specs=[vm, hbm] + [vm] * 12, out_specs=(hbm, hbm, vm, vm),
+        in_specs=[hbm, hbm] + [vm] * 12, out_specs=(hbm, hbm, hbm, vm),
         scratch_shapes=scratches(),
         compiler_params=pltpu.CompilerParams(
             vmem_limit_bytes=int(63.5 * 2**20), collective_id=0, has_side_effects=True),
     )(x, dy, *params)
 
 
-def unpack_body(out_in, ig_in, fin, finv, out, ig, g1, s1, gqkv, gqv, go, bo, g2, s2, gup, bup, gd, bd, sems):
-    copies = [pltpu.make_async_copy(out_in, out, sems.at[0]), pltpu.make_async_copy(ig_in, ig, sems.at[1])]
-    for copy in copies:
+def unpack_body(out_in, ig_in, fin, finv, out, ig, g1, s1, gqkv, gqv, go, bo, g2, s2, gup, bup, gd, bd, held, sems):
+    pairs = ((out_in, out), (ig_in, ig))
+    reads, copies = [], []
+    for j, (src, dst) in enumerate(pairs):
+        for p in range(4):
+            some = pl.ds(3 * p, 3)
+            reads.append(pltpu.make_async_copy(src.at[some], held.at[j, some], sems.at[0, 4 * j + p]))
+            copies.append(pltpu.make_async_copy(held.at[j, some], dst.at[some], sems.at[1, 4 * j + p]))
+    for read in reads:
+        read.start()
+    for read, copy in zip(reads, copies):
+        read.wait()
         copy.start()
     for b in range(12):
         gup[:, 128 * b:128 * b + 128] = fin[UP_ROW + 96 * b:UP_ROW + 96 * b + 96, :].astype(F32)
@@ -552,8 +566,8 @@
         out_shape=(whole, whole, S(96), S(96), S(96, 3 * D), S(192), S(96, D), S(96), S(96), S(96),
                    S(96, FF), S(384), S(384, D), S(96)),
         in_specs=[hbm, hbm, vm, vm], out_specs=(hbm, hbm) + (vm,) * 12,
-        scratch_shapes=[pltpu.SemaphoreType.DMA((2,))],
-        compiler_params=pltpu.CompilerParams(vmem_limit_bytes=24 * 2**20),
+        scratch_shapes=[pltpu.VMEM((2, *outputs.shape), BF16), pltpu.SemaphoreType.DMA((2, 8))],
+        compiler_params=pltpu.CompilerParams(vmem_limit_bytes=62 * 2**20),
     )(outputs, input_grad, fin, finv)
 
 

time: 125 us -> 122 us (0.976)
  local copies, waits for them, and re-layouts: 4.86 us -> 0 us
  Pallas kernels: 118 us -> 121 us
    unnamed x8 -> x0, local copies, waits for them, and re-layouts: 4.86 us -> none
    pallas_call x1, Pallas kernels: 3.1 us -> 5.51 us  [unpack(): pl.pallas_call(unpack_body, out_shape=(whole, whole, S(96), S(96), S(96,...]
where the time goes in v4:
time: 122 us; the launch traced here: 121 us
  Pallas kernels  121 us (99%)
    pallas_call x1, Pallas kernels, layer(): pl.pallas_call(body, out_shape=(S(x.shape, BF16), S(x.shape, BF16), S((GR...  115 us
    pallas_call x1, Pallas kernels, unpack(): pl.pallas_call(unpack_body, out_shape=(whole, whole, S(96), S(96), S(96,...  5.51 us

profile of v4, /device:TPU:2, one launch (start us, length us, event | category | flops | bytes accessed | tf_op | source)
XLA Modules:
  0.0 121.3 jit_solution(8538973725847675622)
XLA Ops:
  0.7 115.0 %shard_map.245 = (bf16[12,197,384]{2,1,0:T(8,128)(2,1)}, bf16[12,197,384]{2,1,0:T(8,128)(2,1)}, bf16[3584,128]{1,0:T(8,128)(2,1)}, bf16[16,128]{1,0:T(8,128)(2,1)}) custom-call(bf16[12,197,384]{2,1,0:T(8,128)(2,1)} %x_in.1, bf16[12,197,384]{2,1,0:T(8,128)(2,1)} %dy_ref.1, bf16[96]{0:T(256)(128)(2,1)} %g1_in.1, bf16[96]{0:T(256)(128)(2,1)} %s1_in.1, ...), custom_call_target="tpu_custom_call" | custom-call | tf_op jit(solution)/shard_map/pallas_call | solution.py:515
  115.7 5.5 %shard_map.246 = (bf16[12,197,384]{2,1,0:T(8,128)(2,1)}, bf16[12,197,384]{2,1,0:T(8,128)(2,1)}, f32[96]{0:T(128)}, f32[96]{0:T(128)}, f32[96,1152]{1,0:T(8,128)}...) custom-call(bf16[12,197,384]{2,1,0:T(8,128)(2,1)} %get-tuple-element, ...), custom_call_target="tpu_custom_call" | custom-call | tf_op jit(solution)/shard_map/pallas_call | solution.py:564

commit v5 on v4

--- a/solution.py
+++ b/solution.py
@@ -334,19 +334,17 @@
         h2s[r, :] = h2
         dy = dys[r, :]
         bup = vcat(9, 4)
-        acc, dh = x1 + vec(5), None
         for f in range(FF // FC):
             fc = slice(f * FC, f * FC + FC)
             u = mm(h2, wup[:, fc]) + bup[:, fc]
+            da = mm_nt(dy, wd[fc, :])
             g, gp = gelu_both(u)
-            g = g.astype(BF16)
-            gs[r, fc] = g
-            acc = acc + mm(g, wd[fc, :])
-            du = (mm_nt(dy, wd[fc, :]) * gp).astype(BF16)
+            gs[r, fc] = g.astype(BF16)
+            du = (da * gp).astype(BF16)
             dus[r, fc] = du
             gub[0:1, fc] += colsum(du.astype(F32))
-            o = mm_nt(du, wup[:, fc])
-            dh = o if dh is None else dh + o
+        acc = x1 + vec(5) + mm(gs[r, :], wd[...])
+        dh = mm_nt(dus[r, :], wup[...])
         for j in range(CH2):
             stage[c * CH2 + j] = acc[j * PAD:j * PAD + SEQ].astype(BF16)
         gvec[3:4, :] += colsum(dh * n2)
@@ -522,7 +520,9 @@
     )(x, dy, *params)
 
 
-def unpack_body(out_in, ig_in, fin, finv, out, ig, g1, s1, gqkv, gqv, go, bo, g2, s2, gup, bup, gd, bd, held, sems):
+def unpack_body(out_in, ig_in, fin_in, finv, out, ig, g1, s1, gqkv, gqv, go, bo, g2, s2, gup, bup, gd, bd, fin, held, fin_sem, sems):
+    fin_copy = pltpu.make_async_copy(fin_in, fin, fin_sem)
+    fin_copy.start()
     pairs = ((out_in, out), (ig_in, ig))
     reads, copies = [], []
     for j, (src, dst) in enumerate(pairs):
@@ -535,6 +535,7 @@
     for read, copy in zip(reads, copies):
         read.wait()
         copy.start()
+    fin_copy.wait()
     for b in range(12):
         gup[:, 128 * b:128 * b + 128] = fin[UP_ROW + 96 * b:UP_ROW + 96 * b + 96, :].astype(F32)
     for b in range(3):
@@ -565,8 +566,9 @@
         unpack_body,
         out_shape=(whole, whole, S(96), S(96), S(96, 3 * D), S(192), S(96, D), S(96), S(96), S(96),
                    S(96, FF), S(384), S(384, D), S(96)),
-        in_specs=[hbm, hbm, vm, vm], out_specs=(hbm, hbm) + (vm,) * 12,
-        scratch_shapes=[pltpu.VMEM((2, *outputs.shape), BF16), pltpu.SemaphoreType.DMA((2, 8))],
+        in_specs=[hbm, hbm, hbm, vm], out_specs=(hbm, hbm) + (vm,) * 12,
+        scratch_shapes=[pltpu.VMEM(fin.shape, BF16), pltpu.VMEM((2, *outputs.shape), BF16), pltpu.SemaphoreType.DMA,
+                        pltpu.SemaphoreType.DMA((2, 8))],
         compiler_params=pltpu.CompilerParams(vmem_limit_bytes=62 * 2**20),
     )(outputs, input_grad, fin, finv)
 

time: 122 us -> 122 us (level)
  no operation moved by 1% of the time
where the time goes in v5:
time: 122 us; the launch traced here: 121 us
  Pallas kernels  120 us (98%)
    pallas_call x1, Pallas kernels, layer(): pl.pallas_call(body, out_shape=(S(x.shape, BF16), S(x.shape, BF16), S((GR...  115 us
    pallas_call x1, Pallas kernels, unpack(): pl.pallas_call(unpack_body, out_shape=(whole, whole, S(96), S(96), S(96,...  5.97 us

profile of v5, /device:TPU:2, one launch (start us, length us, event | category | flops | bytes accessed | tf_op | source)
XLA Modules:
  0.0 121.3 jit_solution(2864067028879373142)
XLA Ops:
  0.7 114.5 %shard_map.245 = (bf16[12,197,384]{2,1,0:T(8,128)(2,1)}, bf16[12,197,384]{2,1,0:T(8,128)(2,1)}, bf16[3584,128]{1,0:T(8,128)(2,1)}, bf16[16,128]{1,0:T(8,128)(2,1)}) custom-call(bf16[12,197,384]{2,1,0:T(8,128)(2,1)} %x_in.1, bf16[12,197,384]{2,1,0:T(8,128)(2,1)} %dy_ref.1, bf16[96]{0:T(256)(128)(2,1)} %g1_in.1, bf16[96]{0:T(256)(128)(2,1)} %s1_in.1, ...), custom_call_target="tpu_custom_call" | custom-call | tf_op jit(solution)/shard_map/pallas_call | solution.py:513
  115.2 6.0 %shard_map.246 = (bf16[12,197,384]{2,1,0:T(8,128)(2,1)}, bf16[12,197,384]{2,1,0:T(8,128)(2,1)}, f32[96]{0:T(128)}, f32[96]{0:T(128)}, f32[96,1152]{1,0:T(8,128)}...) custom-call(bf16[12,197,384]{2,1,0:T(8,128)(2,1)} %get-tuple-element, ...), custom_call_target="tpu_custom_call" | custom-call | tf_op jit(solution)/shard_map/pallas_call | solution.py:565
